TPU v7x, 256 devices: a whole 4x4x8 slice. The times are simulated.
256 devices in a mesh: row: 16 (over z_hi, x, core), col: 16 (over z_lo, y).
Axes of the slice: x: 4, y: 4, z: 8 (z_hi: 2, z_lo: 4; z = z_hi * 4 + z_lo), core: 2. Of those that a mesh axis runs over, the one named last changes fastest.
Arguments:
- queries: bfloat16 [131072, 768], P(('row', 'col')), may hold values from -52 to 52
- keys: bfloat16 [131072, 768], P(('row', 'col')), may hold values from -6 to 6
- values: bfloat16 [131072, 768], P(('row', 'col')), may hold values from -6 to 6
- out_weight: bfloat16 [768, 768], replicated, may hold values from -0.21875 to 0.21875
Outputs:
- layer_out: bfloat16 [131072, 768], P(('row', 'col'))
All inputs are finite; a program needn't handle non-finite values.
Results may differ from a plain program's by a relative error of at most 0.0015.
The roundings to bfloat16 on the way count: a program that leaves them out, or rounds other values in their place, can miss the bound.
Values may be sent and summed in bfloat16 or wider, within the bound.
No kernel may reach another device: no remote copies, remote signals or barrier semaphores. Data moves between devices by JAX's collectives and lax.ppermute only.
A program may use at most 64 MiB of HBM per device.

v0:
```python
import jax
import jax.numpy as jnp
import numpy as np
from jax import lax
from jax.sharding import PartitionSpec as P

HEADS = 12


def attend(query_rows, key_rows, value_rows):
    score_scale = query_rows.shape[-1] ** (-0.5)
    scores = (
        jnp.einsum("qhd,khd->hqk", query_rows, key_rows, preferred_element_type=jnp.float32)
        * score_scale
    )
    row_max = jnp.max(scores, axis=-1, keepdims=True)
    exponent = jnp.exp(scores - row_max)
    totals = jnp.sum(exponent, axis=-1)
    weights = exponent.astype(jnp.bfloat16)
    summed = jnp.einsum("hqk,khd->qhd", weights, value_rows, preferred_element_type=jnp.float32)
    outputs = summed / jnp.transpose(totals)[:, :, None]
    return (outputs, jnp.transpose(row_max[..., 0] + jnp.log(totals)))


def spread(compact, period, offsets, filler):
    chosen = jnp.arange(period)[:, None] == jnp.asarray(offsets)[None, :]
    if compact.ndim == 3:
        chosen = chosen[None, :, :, None]
    else:
        chosen = chosen[None, :, :]
    placed = jnp.where(chosen, compact[:, None], filler)
    return placed.reshape((-1,) + compact.shape[1:])


def combine(pieces):
    row_max = pieces[0][1]
    for piece in pieces[1:]:
        row_max = jnp.maximum(row_max, piece[1])
    numer = jnp.zeros_like(pieces[0][0])
    denom = jnp.zeros_like(row_max)
    for piece in pieces:
        factor = jnp.exp(piece[1] - row_max)
        numer = numer + factor[:, :, None] * piece[0]
        denom = denom + factor
    return numer / denom[:, :, None]


def shards(queries, keys, values, out_weight):
    row_count = lax.axis_size("row")
    col_count = lax.axis_size("col")
    top_period = row_count * col_count
    tok_rows, model_width = queries.shape
    head_count = HEADS
    head_dim = model_width // head_count
    head_ids = np.arange(head_count)
    first_offsets = head_ids % col_count
    second_offsets = head_ids % top_period
    query_heads = queries.reshape(tok_rows, head_count, head_dim)
    key_heads = keys.reshape(tok_rows, head_count, head_dim)
    value_heads = values.reshape(tok_rows, head_count, head_dim)

    def select_rows(source, period, offsets):
        return source.reshape(tok_rows // period, period, head_count, head_dim)[
            :, offsets, head_ids
        ]

    seg_keys, seg_values = (
        lax.all_gather(
            select_rows(key_heads, col_count, first_offsets).reshape(-1, model_width),
            "col",
            axis=0,
            tiled=True,
        ),
        lax.all_gather(
            select_rows(value_heads, col_count, first_offsets).reshape(-1, model_width),
            "col",
            axis=0,
            tiled=True,
        ),
    )
    block_out, block_lse = attend(query_heads, key_heads, value_heads)
    gathered_keys = seg_keys.reshape(tok_rows, head_count, head_dim)
    gathered_values = seg_values.reshape(tok_rows, head_count, head_dim)
    out_one, lse_one = attend(
        select_rows(query_heads, col_count, first_offsets), gathered_keys, gathered_values
    )
    top_keys, top_values = (
        lax.all_gather(
            select_rows(key_heads, top_period, second_offsets).reshape(-1, model_width),
            ("row", "col"),
            axis=0,
            tiled=True,
        ),
        lax.all_gather(
            select_rows(value_heads, top_period, second_offsets).reshape(-1, model_width),
            ("row", "col"),
            axis=0,
            tiled=True,
        ),
    )
    out_two, lse_two = attend(
        select_rows(query_heads, top_period, second_offsets),
        top_keys.reshape(tok_rows, head_count, head_dim),
        top_values.reshape(tok_rows, head_count, head_dim),
    )
    first_full = spread(out_one, col_count, first_offsets, 0.0)
    first_lse = spread(lse_one, col_count, first_offsets, -jnp.inf)
    second_full = spread(out_two, top_period, second_offsets, 0.0)
    second_lse = spread(lse_two, top_period, second_offsets, -jnp.inf)
    mixed = combine([(block_out, block_lse), (first_full, first_lse), (second_full, second_lse)])
    mixed = mixed.astype(jnp.bfloat16).reshape(tok_rows, model_width)
    return jnp.dot(mixed, out_weight, preferred_element_type=jnp.float32).astype(jnp.bfloat16)


def solution(mesh):
    placed = (P(("row", "col"), None), P(("row", "col"), None), P(("row", "col"), None), P())
    return jax.shard_map(
        shards, mesh=mesh, in_specs=placed, out_specs=P(("row", "col"), None), check_vma=False
    )
```

profile of v0, /device:TPU:8, one launch (start us, length us, event | category | flops | bytes accessed | tf_op | source)
XLA Modules:
  0.0 1424.7 jit_solution(1650294997013309886)
XLA Ops:
  0.0 0.0 copy-start
  0.0 1.5 copy.84
  1.5 0.0 copy-start.6
  1.5 0.2 reshape_reshape.23
  1.7 3.3 copy.91
  5.1 0.0 copy-done.6
  5.1 2.1 gather_fusion.5
  7.1 0.1 reshape.192
  7.2 627.2 %all-gather.1 = bf16[256,2,768]{2,1,0:T(2,128)(2,1)S(1)} all-gather(bf16[1,2,768]{2,1,0:T(2,128)(2,1)S(1)} %reshape.192), channel_id=1, replica_groups=mesh['row'=16,'col'=16] {'row','col'}, dimensions={0}, use_global_device_ids=true | all-gather | bytes 789504 | tf_op jit(solution)/shard_map/all_gather | solution.py:94
  634.4 2.2 reshape.152
  636.6 0.0 copy-done.8
  636.6 0.3 copy.73
  636.9 0.0 copy-start.2
  636.9 0.2 reshape_reshape.21
  637.1 3.3 copy.81
  640.4 0.0 copy-done.2
  640.4 2.1 gather_fusion.3
  642.4 0.1 reshape.190
  642.5 629.9 %all-gather = bf16[256,2,768]{2,1,0:T(2,128)(2,1)S(1)} all-gather(bf16[1,2,768]{2,1,0:T(2,128)(2,1)S(1)} %reshape.190), channel_id=1, replica_groups=mesh['row'=16,'col'=16] {'row','col'}, dimensions={0}, use_global_device_ids=true | all-gather | bytes 789504 | tf_op jit(solution)/shard_map/all_gather | solution.py:88
  1272.4 2.1 reshape.147
  1274.5 0.0 copy-done.9
  1274.5 0.3 copy.72
  1274.8 0.0 copy-start.4
  1274.8 0.2 reshape_reshape.20
  1275.0 3.3 copy.79
  1278.3 0.0 copy-done.4
  1278.3 2.1 gather_fusion.2
  1280.3 2.3 fusion.46
  1282.7 0.2 fusion.33
  1282.8 2.2 fusion.24
  1285.0 0.2 copy.94
  1285.2 1.0 broadcast_in_dim.176
  1286.2 2.5 broadcast_in_dim.177
  1288.6 2.7 reshape_reshape.22
  1291.4 2.2 copy.86
  1293.6 2.0 gather_fusion.4
  1295.7 0.1 reshape.149
  1295.8 41.6 %all_gather.14 = bf16[512,768]{1,0:T(8,128)(2,1)S(1)} all-gather(bf16[32,768]{1,0:T(8,128)(2,1)S(1)} %reshape.149), channel_id=1, replica_groups=mesh['row'=16,'col'=16] {'col'}, dimensions={0}, use_global_device_ids=true | all-gather | bytes 835584 | tf_op jit(solution)/shard_map/all_gather | solution.py:74
  1337.4 1.2 copy.88
  1338.6 2.7 reshape_reshape.19
  1341.3 2.2 copy.75
  1343.5 2.0 gather_fusion.1
  1345.6 0.1 reshape.144
  1345.7 42.4 %all_gather.12 = bf16[512,768]{1,0:T(8,128)(2,1)S(1)} all-gather(bf16[32,768]{1,0:T(8,128)(2,1)S(1)} %reshape.144), channel_id=1, replica_groups=mesh['row'=16,'col'=16] {'col'}, dimensions={0}, use_global_device_ids=true | all-gather | bytes 835584 | tf_op jit(solution)/shard_map/all_gather | solution.py:68
  1388.1 1.1 copy.77
  1389.2 2.7 reshape_reshape.18
  1391.9 2.2 copy.74
  1394.1 2.1 gather_fusion
  1396.2 1.5 fusion.47
  1397.7 0.3 fusion.28
  1398.0 0.0 copy-done.10
  1398.0 0.4 fusion.17
  1398.4 1.9 broadcast_in_dim.170
  1400.3 3.3 copy.89
  1403.6 0.0 copy-done.3
  1403.7 6.4 multiply_reduce_fusion
  1410.1 0.2 broadcast_in_dim.151
  1410.3 0.1 broadcast_in_dim.156
  1410.4 0.1 broadcast_in_dim.157
  1410.5 6.8 fusion.1
  1417.5 0.1 broadcast_bitcast_fusion.1
  1417.6 1.1 copy-done.1
  1418.7 4.2 fusion.14
  1423.0 1.7 convolution_convert_fusion
  (27 shorter events, 0.3 us)
Async XLA Ops:
  0.0 1423.0 %copy-start = (bf16[768,768]{1,0:T(8,128)(2,1)S(1)}, bf16[768,768]{1,0:T(8,128)(2,1)}, u32[]{:S(2)}) copy-start(bf16[768,768]{1,0:T(8,128)(2,1)} %param.22) | copy-start | bytes 3538948
  1.5 3.5 copy-start.6
  634.4 2.2 copy-start.8
  636.9 3.5 copy-start.2
  1272.4 2.1 copy-start.9
  1274.8 3.5 copy-start.4
  1394.1 3.9 copy-start.10
  1400.3 3.4 copy-start.3
  1400.3 3.4 copy-start.5
  1410.3 7.4 copy-start.7
  1410.5 8.2 copy-start.1
where the time goes:
time: 1430 us; the launch traced here: 1420 us
  blocking collectives  1340 us (94%)
  local copies, waits for them, and re-layouts  57.3 us (4%)
  matrix products  18.7 us (1%)
    all_gather x1, blocking collectives, shards(): lax.all_gather(select_rows(key_heads, top_period, second_offsets).reshape...  630 us
    all_gather x1, blocking collectives, shards(): lax.all_gather(select_rows(value_heads, top_period, second_offsets).resha...  627 us
    all_gather x1, blocking collectives, shards(): lax.all_gather(select_rows(key_heads, col_count, first_offsets).reshape(-...  42.4 us
    all_gather x1, blocking collectives, shards(): lax.all_gather(select_rows(value_heads, col_count, first_offsets).reshape...  41.6 us

commit v1 on v0

v1 whole, which is shorter than its diff:
```python
import jax
import jax.numpy as jnp
from jax import lax
from jax.experimental import pallas as pl
from jax.experimental.pallas import tpu as pltpu
from jax.sharding import PartitionSpec as P

HEADS = 12
F32 = jnp.float32
BF16 = jnp.bfloat16
NT = (((1,), (1,)), ((), ()))


def lane_is_low(shape):
    return lax.broadcasted_iota(jnp.int32, shape, len(shape) - 1) < 64


def swap(block):
    return pltpu.roll(block, 64, block.ndim - 1)


def chosen_lanes(period, width):
    offset = lax.broadcasted_iota(jnp.int32, (period, width), 0)
    head = lax.broadcasted_iota(jnp.int32, (period, width), 1) // 64
    return offset == head


def pack_kernel(period, q_ref, k_ref, v_ref, x_ref):
    rows, width = q_ref.shape
    groups = rows // period
    keep = chosen_lanes(period, width).astype(BF16)
    member = (
        lax.broadcasted_iota(jnp.int32, (groups, rows), 1) // period
        == lax.broadcasted_iota(jnp.int32, (groups, rows), 0)
    ).astype(BF16)

    def pick(ref):
        kept = ref[...].reshape(groups, period, width) * keep[None]
        return jnp.dot(member, kept.reshape(rows, width), preferred_element_type=F32)

    q, k, v = pick(q_ref), pick(k_ref), pick(v_ref)
    low = lane_is_low((groups, 128))
    low_half = lane_is_low((groups // 2, 128))
    for pair in range(HEADS // 2):
        lanes = slice(pair * 128, pair * 128 + 128)
        qb, kb, vb = q[:, lanes], k[:, lanes], v[:, lanes]
        top, bottom = vb[: groups // 2], vb[groups // 2 :]
        x_ref[2 * pair, :groups] = jnp.where(low, qb, swap(kb)).astype(BF16)
        x_ref[2 * pair, groups:] = jnp.where(low_half, top, swap(bottom)).astype(BF16)
        x_ref[2 * pair + 1, :groups] = jnp.where(low, swap(qb), kb).astype(BF16)
        x_ref[2 * pair + 1, groups:] = jnp.where(low_half, swap(top), bottom).astype(BF16)
    for rest in range(HEADS, x_ref.shape[0]):
        x_ref[rest] = jnp.zeros(x_ref.shape[1:], BF16)


def middle_kernel(y_ref, z_ref):
    y = y_ref[...].astype(F32)
    first, second, val = y[:, 0, :], y[:, 16, :], y[:, 32, :]
    low = lane_is_low(first.shape)
    top = jnp.where(low, swap(first), swap(val)).astype(BF16)
    bottom = jnp.where(low, swap(second), val).astype(BF16)
    both = jnp.concatenate([top, bottom], axis=0)
    for i in range(z_ref.shape[0]):
        z_ref[i] = both


def soft(scores):
    top = jnp.max(scores, axis=-1, keepdims=True)
    weights = jnp.exp((scores - top) * 0.125)
    total = jnp.sum(weights, axis=-1, keepdims=True)
    return weights.astype(BF16), total, top * 0.125 + jnp.log(total)


def merge(out_a, lse_a, out_b, lse_b):
    top = jnp.maximum(lse_a, lse_b)
    wa, wb = jnp.exp(lse_a - top), jnp.exp(lse_b - top)
    total = wa + wb
    return (wa * out_a + wb * out_b) / total, top + jnp.log(total)


def shared_kernel(y_ref, z_ref, ret_ref):
    n, _, _ = y_ref.shape
    qk = y_ref[:, :32, :].reshape(n * 32, 128).astype(F32)
    low = lane_is_low(qk.shape)
    query = jnp.where(low, qk, 0.0).astype(BF16)
    key = swap(qk).astype(BF16)
    val = y_ref[:, 32:, :].astype(F32).reshape(n * 16, 128)
    other = swap(val).reshape(n, 16, 128)
    val = jnp.concatenate([val.reshape(n, 16, 128), other], axis=1).reshape(n * 32, 128).astype(BF16)
    scores = lax.dot_general(query, key, NT, preferred_element_type=F32)
    probs, total, lse = soft(scores)
    out = jnp.dot(probs, val, preferred_element_type=F32) / total
    ret_ref[...] = jnp.where(low, out, lse).reshape(n, 32, 128)

    y = y_ref[...].astype(F32)
    q2 = jnp.concatenate([y[:, 0, :], y[:, 16, :]], axis=0)
    low2 = lane_is_low(q2.shape)
    q2 = jnp.where(low2, q2, 0.0).astype(BF16)
    kv = z_ref[...].reshape(-1, 128)
    scores2 = lax.dot_general(q2, kv, NT, preferred_element_type=F32)
    probs2, total2, lse2 = soft(scores2)
    out2 = swap(jnp.dot(probs2, kv, preferred_element_type=F32) / total2)
    for i in range(2):
        old = ret_ref[:, 16 * i, :]
        part = slice(n * i, n * i + n)
        lse_old = swap(old)
        mixed, lse_new = merge(old, lse_old, out2[part], lse2[part])
        lown = lane_is_low(old.shape)
        ret_ref[:, 16 * i, :] = jnp.where(lown, mixed, swap(lse_new))


def local_kernel(q_ref, k_ref, v_ref, o_ref, s_ref, out_scr, lse_scr):
    pair = pl.program_id(0)
    q, k, v = q_ref[...], k_ref[...], v_ref[...]
    low = lane_is_low(q.shape)
    outs, lses = [], []
    for half in range(2):
        query = jnp.where(low == (half == 0), q, jnp.zeros_like(q))
        scores = lax.dot_general(query, k, NT, preferred_element_type=F32)
        probs, total, lse = soft(scores)
        outs.append(jnp.dot(probs, v, preferred_element_type=F32) / total)
        lses.append(lse)
    out = jnp.where(low, outs[0], outs[1])
    o_ref[...] = out.astype(BF16)
    out_scr[...] = out
    lse_scr[...] = jnp.where(low, lses[0], lses[1])
    for half in range(2):
        rows = pl.ds(2 * pair + half, s_ref.shape[1], stride=16)
        o, l = out_scr[rows, :], lse_scr[rows, :]
        lowr = lane_is_low(o.shape)
        if half == 0:
            s_ref[half] = jnp.where(lowr, o, swap(l))
        else:
            s_ref[half] = jnp.where(lowr, swap(o), l)


def finish_kernel(period, o_ref, s_ref, r_ref, w_ref, out_ref):
    rows, width = o_ref.shape
    groups = rows // period
    low = lane_is_low((groups, 128))
    blocks = []
    for pair in range(HEADS // 2):
        halves = []
        for half in range(2):
            a, b = s_ref[2 * pair + half], r_ref[2 * pair + half]
            halves.append(merge(a, swap(a), b, swap(b))[0])
        blocks.append(jnp.where(low, halves[0], swap(halves[1])).astype(BF16))
    merged = jnp.concatenate(blocks, axis=1)
    member = (
        lax.broadcasted_iota(jnp.int32, (rows, groups), 0) // period
        == lax.broadcasted_iota(jnp.int32, (rows, groups), 1)
    ).astype(BF16)
    spread = jnp.dot(member, merged, preferred_element_type=F32).reshape(groups, period, width)
    keep = chosen_lanes(period, width)[None]
    local = o_ref[...].astype(F32).reshape(groups, period, width)
    mixed = jnp.where(keep, spread, local).reshape(rows, width).astype(BF16)
    out_ref[...] = jnp.dot(mixed, w_ref[...], preferred_element_type=F32).astype(BF16)


def shards(queries, keys, values, out_weight):
    n_row, n_col = lax.axis_size("row"), lax.axis_size("col")
    rows, width = queries.shape
    groups = rows // n_col
    params = pltpu.CompilerParams(vmem_limit_bytes=48 * 1024 * 1024)

    def call(kernel, out, **kw):
        return pl.pallas_call(kernel, out_shape=out, compiler_params=params, **kw)

    shape = jax.ShapeDtypeStruct
    packed = call(
        lambda *refs: pack_kernel(n_col, *refs), shape((n_col, groups * 3 // 2, 128), BF16)
    )(queries, keys, values)
    mine = lax.all_to_all(packed, "col", 0, 0)
    top_own = call(middle_kernel, shape((n_row, 2 * n_col, 128), BF16))(mine)
    top_all = lax.all_to_all(top_own, "row", 0, 0)
    block = pl.BlockSpec((rows, 128), lambda i: (0, i))
    local, picked = call(
        local_kernel,
        (shape((rows, width), BF16), shape((HEADS, groups, 128), F32)),
        grid=(HEADS // 2,),
        in_specs=[block] * 3,
        out_specs=(block, pl.BlockSpec((2, groups, 128), lambda i: (i, 0, 0))),
        scratch_shapes=[pltpu.VMEM((rows, 128), F32)] * 2,
    )(queries, keys, values)
    ret = call(shared_kernel, shape((n_col, groups, 128), F32))(mine, top_all)
    back = lax.all_to_all(ret, "col", 0, 0)
    return call(
        lambda *refs: finish_kernel(n_col, *refs), shape((rows, width), BF16)
    )(local, picked, back, out_weight)


def solution(mesh):
    placed = (P(("row", "col"), None), P(("row", "col"), None), P(("row", "col"), None), P())
    return jax.shard_map(
        shards, mesh=mesh, in_specs=placed, out_specs=P(("row", "col"), None), check_vma=False
    )
```

time: 1430 us -> 63.3 us (0.04)
  the two profiles are of different devices: /device:TPU:8 before, /device:TPU:1 now
where the time goes in v1:
time: 63.3 us; the launch traced here: 62.8 us
  blocking collectives  37.8 us (60%)
  Pallas kernels  13 us (21%)
  local copies, waits for them, and re-layouts  7.03 us (11%)
  starting transfers between devices  4.2 us (7%)
  waiting for transfers between devices  0.72 us (1%)
    all_to_all x1, blocking collectives, shards(): top_all = lax.all_to_all(top_own, 'row', 0, 0)  20.3 us
    all_to_all x1, blocking collectives, shards(): mine = lax.all_to_all(packed, 'col', 0, 0)  17.5 us
    pallas_call x1, Pallas kernels, shards(): call(local_kernel, (shape((rows, width), BF16), shape((HEADS, groups, 128...  7.58 us
    unnamed x22, local copies, waits for them, and re-layouts  7.03 us
    all_to_all x1, starting transfers between devices, shards(): back = lax.all_to_all(ret, 'col', 0, 0)  4.2 us
    pallas_call x1, Pallas kernels, shards(): call(lambda *refs: finish_kernel(n_col, *refs), shape((rows, width), BF16))  2.97 us
    pallas_call x1, Pallas kernels, shards(): ret = call(shared_kernel, shape((n_col, groups, 128), F32))(mine, top_all)  1.72 us
  transfers between devices with their start and end apart: 1, of which 1 were waited for; matrix products, arithmetic and copies ran while one was open for 0% of the time, Pallas kernels for 12%

profile of v1, /device:TPU:1, one launch (start us, length us, event | category | flops | bytes accessed | tf_op | source)
XLA Modules:
  0.0 62.8 jit_solution(3799737163323958562)
XLA Ops:
  0.0 0.0 copy-start
  0.0 1.1 %copy-done = bf16[512,768]{1,0:T(8,128)(2,1)S(1)} copy-done((bf16[512,768]{1,0:T(8,128)(2,1)S(1)}, bf16[512,768]{1,0:T(8,128)(2,1)}, u32[]{:S(2)}) %copy-start) | copy-done | bytes 786456
  1.1 0.0 copy-start.2
  1.1 1.1 %copy-done.2 = bf16[512,768]{1,0:T(8,128)(2,1)S(1)} copy-done((bf16[512,768]{1,0:T(8,128)(2,1)S(1)}, bf16[512,768]{1,0:T(8,128)(2,1)}, u32[]{:S(2)}) %copy-start.2) | copy-done | bytes 786456
  2.3 0.0 copy-start.4
  2.3 1.1 %copy-done.4 = bf16[512,768]{1,0:T(8,128)(2,1)S(1)} copy-done((bf16[512,768]{1,0:T(8,128)(2,1)S(1)}, bf16[512,768]{1,0:T(8,128)(2,1)}, u32[]{:S(2)}) %copy-start.4) | copy-done | bytes 786456
  3.4 0.0 copy-start.5
  3.4 0.6 shard_map.47
  4.0 0.0 copy-start.1
  4.0 0.0 copy-start.3
  4.0 17.5 %all_to_all.15.y_ref = bf16[16,48,128]{2,1,0:T(8,128)(2,1)S(1)} all-to-all(bf16[16,48,128]{2,1,0:T(8,128)(2,1)S(1)} %shard_map.47), channel_id=1, replica_groups=mesh['row'=16,'col'=16] {'col'}, dimensions={0} | all-to-all | bytes 393216 | tf_op jit(solution)/shard_map/all_to_all | solution.py:173
  21.6 0.1 shard_map.48
  21.7 20.3 %all_to_all.16.z_ref = bf16[16,32,128]{2,1,0:T(8,128)(2,1)S(1)} all-to-all(bf16[16,32,128]{2,1,0:T(8,128)(2,1)S(1)} %shard_map.48), channel_id=1, replica_groups=mesh['row'=16,'col'=16] {'row'}, dimensions={0} | all-to-all | bytes 262144 | tf_op jit(solution)/shard_map/all_to_all | solution.py:175
  41.9 1.7 %shard_map.49 = f32[16,32,128]{2,1,0:T(8,128)} custom-call(bf16[16,48,128]{2,1,0:T(8,128)(2,1)S(1)} %all_to_all.15.y_ref, bf16[16,32,128]{2,1,0:T(8,128)(2,1)S(1)} %all_to_all.16.z_ref), custom_call_target="tpu_custom_call" | custom-call | tf_op jit(solution)/shard_map/pallas_call | solution.py:185
  43.6 4.2 %all-to-all-start.2 = ((f32[16,32,128]{2,1,0:T(8,128)}), f32[16,32,128]{2,1,0:T(8,128)}, u32[]{:S(2)}, u32[]{:S(2)}) async-start(f32[16,32,128]{2,1,0:T(8,128)} %shard_map.49), calls=%async_computation.2 | async-start | bytes 524288 | tf_op jit(solution)/shard_map/all_to_all | solution.py:186
  47.8 0.0 copy-done.5
  47.9 0.0 copy-done.1
  47.9 0.0 copy-done.3
  47.9 0.0 copy-start.6
  47.9 7.6 %shard_map.46 = (bf16[512,768]{1,0:T(8,128)(2,1)S(1)}, f32[12,32,128]{2,1,0:T(8,128)S(1)}) custom-call(bf16[512,768]{1,0:T(8,128)(2,1)S(1)} %copy-done.1, bf16[512,768]{1,0:T(8,128)(2,1)S(1)} %copy-done.3, bf16[512,768]{1,0:T(8,128)(2,1)S(1)} %copy-done.5), custom_call_target="tpu_custom_call" | custom-call | tf_op jit(solution)/shard_map/pallas_call | solution.py:177
  55.5 0.0 copy-start.7
  55.5 0.9 %copy-done.7 = bf16[512,768]{1,0:T(8,128)(2,1)} copy-done((bf16[512,768]{1,0:T(8,128)(2,1)}, bf16[512,768]{1,0:T(8,128)(2,1)S(1)}, u32[]{:S(2)}) %copy-start.7) | copy-done | bytes 786456
  56.4 0.0 copy-start.9
  56.4 0.7 %copy-done.9 = f32[12,32,128]{2,1,0:T(8,128)} copy-done((f32[12,32,128]{2,1,0:T(8,128)}, f32[12,32,128]{2,1,0:T(8,128)S(1)}, u32[]{:S(2)}) %copy-start.9) | copy-done | bytes 196632
  57.0 0.7 %all-to-all-done.2.refs_2_ = f32[16,32,128]{2,1,0:T(8,128)} async-done(((f32[16,32,128]{2,1,0:T(8,128)}), f32[16,32,128]{2,1,0:T(8,128)}, u32[]{:S(2)}, u32[]{:S(2)}) %all-to-all-start.2) | async-done | bytes 262176 | tf_op jit(solution)/shard_map/all_to_all | solution.py:186
  57.7 0.0 copy-done.6
  57.7 0.0 copy-start.8
  57.8 1.1 %copy-done.8 = bf16[512,768]{1,0:T(8,128)(2,1)S(1)} copy-done((bf16[512,768]{1,0:T(8,128)(2,1)S(1)}, bf16[512,768]{1,0:T(8,128)(2,1)}, u32[]{:S(2)}) %copy-start.8) | copy-done | bytes 786456
  58.9 0.0 copy-start.10
  58.9 0.9 %copy-done.10 = f32[12,32,128]{2,1,0:T(8,128)S(1)} copy-done((f32[12,32,128]{2,1,0:T(8,128)S(1)}, f32[12,32,128]{2,1,0:T(8,128)}, u32[]{:S(2)}) %copy-start.10) | copy-done | bytes 196632
  59.8 3.0 %shard_map.50 = bf16[512,768]{1,0:T(8,128)(2,1)} custom-call(bf16[512,768]{1,0:T(8,128)(2,1)S(1)} %copy-done.8, f32[12,32,128]{2,1,0:T(8,128)S(1)} %copy-done.10, f32[16,32,128]{2,1,0:T(8,128)} %all-to-all-done.2.refs_2_, bf16[768,768]{1,0:T(8,128)(2,1)S(1)} %copy-done.6), custom_call_target="tpu_custom_call" | custom-call | tf_op jit(solution)/shard_map/pallas_call | solution.py:187
Async XLA Ops:
  0.0 1.1 %copy-start = (bf16[512,768]{1,0:T(8,128)(2,1)S(1)}, bf16[512,768]{1,0:T(8,128)(2,1)}, u32[]{:S(2)}) copy-start(bf16[512,768]{1,0:T(8,128)(2,1)} %refs_0_.1) | copy-start | bytes 2359300
  1.1 1.1 %copy-start.2 = (bf16[512,768]{1,0:T(8,128)(2,1)S(1)}, bf16[512,768]{1,0:T(8,128)(2,1)}, u32[]{:S(2)}) copy-start(bf16[512,768]{1,0:T(8,128)(2,1)} %refs_1_.1) | copy-start | bytes 2359300
  2.3 1.1 %copy-start.4 = (bf16[512,768]{1,0:T(8,128)(2,1)S(1)}, bf16[512,768]{1,0:T(8,128)(2,1)}, u32[]{:S(2)}) copy-start(bf16[512,768]{1,0:T(8,128)(2,1)} %refs_2_.1) | copy-start | bytes 2359300
  3.4 44.4 %copy-start.5 = (bf16[512,768]{1,0:T(8,128)(2,1)S(1)}, bf16[512,768]{1,0:T(8,128)(2,1)}, u32[]{:S(2)}) copy-start(bf16[512,768]{1,0:T(8,128)(2,1)} %refs_2_.1) | copy-start | bytes 2359300
  4.0 43.8 %copy-start.1 = (bf16[512,768]{1,0:T(8,128)(2,1)S(1)}, bf16[512,768]{1,0:T(8,128)(2,1)}, u32[]{:S(2)}) copy-start(bf16[512,768]{1,0:T(8,128)(2,1)} %refs_0_.1) | copy-start | bytes 2359300
  4.0 43.8 %copy-start.3 = (bf16[512,768]{1,0:T(8,128)(2,1)S(1)}, bf16[512,768]{1,0:T(8,128)(2,1)}, u32[]{:S(2)}) copy-start(bf16[512,768]{1,0:T(8,128)(2,1)} %refs_1_.1) | copy-start | bytes 2359300
  43.6 14.1 %all-to-all-start.2 = ((f32[16,32,128]{2,1,0:T(8,128)}), f32[16,32,128]{2,1,0:T(8,128)}, u32[]{:S(2)}, u32[]{:S(2)}) async-start(f32[16,32,128]{2,1,0:T(8,128)} %shard_map.49), calls=%async_computation.2 | async-start | bytes 524288 | tf_op jit(solution)/shard_map/all_to_all | solution.py:186
  47.9 9.9 %copy-start.6 = (bf16[768,768]{1,0:T(8,128)(2,1)S(1)}, bf16[768,768]{1,0:T(8,128)(2,1)}, u32[]{:S(2)}) copy-start(bf16[768,768]{1,0:T(8,128)(2,1)} %refs_3_.1) | copy-start | bytes 3538948
  55.5 0.9 %copy-start.7 = (bf16[512,768]{1,0:T(8,128)(2,1)}, bf16[512,768]{1,0:T(8,128)(2,1)S(1)}, u32[]{:S(2)}) copy-start(bf16[512,768]{1,0:T(8,128)(2,1)S(1)} %get-tuple-element.7.refs_0_) | copy-start | bytes 2359300
  56.4 0.7 %copy-start.9 = (f32[12,32,128]{2,1,0:T(8,128)}, f32[12,32,128]{2,1,0:T(8,128)S(1)}, u32[]{:S(2)}) copy-start(f32[12,32,128]{2,1,0:T(8,128)S(1)} %get-tuple-element.8.refs_1_) | copy-start | bytes 589828
  57.7 1.1 %copy-start.8 = (bf16[512,768]{1,0:T(8,128)(2,1)S(1)}, bf16[512,768]{1,0:T(8,128)(2,1)}, u32[]{:S(2)}) copy-start(bf16[512,768]{1,0:T(8,128)(2,1)} %copy-done.7) | copy-start | bytes 2359300
  58.9 0.9 %copy-start.10 = (f32[12,32,128]{2,1,0:T(8,128)S(1)}, f32[12,32,128]{2,1,0:T(8,128)}, u32[]{:S(2)}) copy-start(f32[12,32,128]{2,1,0:T(8,128)} %copy-done.9) | copy-start | bytes 589828

commit v2 on v1

v2 whole, which is shorter than its diff:
```python
import jax
import jax.numpy as jnp
from jax import lax
from jax.experimental import pallas as pl
from jax.experimental.pallas import tpu as pltpu
from jax.sharding import PartitionSpec as P

HEADS = 12
F32 = jnp.float32
BF16 = jnp.bfloat16
NT = (((1,), (1,)), ((), ()))


def lane_is_low(shape):
    return lax.broadcasted_iota(jnp.int32, shape, len(shape) - 1) < 64


def swap(block):
    return pltpu.roll(block, 64, block.ndim - 1)


def chosen_lanes(period, width):
    offset = lax.broadcasted_iota(jnp.int32, (period, width), 0)
    head = lax.broadcasted_iota(jnp.int32, (period, width), 1) // 64
    return offset == head


def slot_of(head, n_row, n_col):
    moved = lax.div(lax.axis_index("row"), n_row // 2) * (n_col // 2)
    return lax.rem(head + moved, n_col)


def pack_kernel(period, n_row, q_hbm, k_hbm, v_hbm, x_ref, buf, sem):
    rows, width = q_hbm.shape
    copies = [
        pltpu.make_async_copy(hbm, buf.at[i], sem.at[i])
        for i, hbm in enumerate((q_hbm, k_hbm, v_hbm))
    ]
    for copy in copies:
        copy.start()
    groups = rows // period
    keep = chosen_lanes(period, width).astype(BF16)
    member = (
        lax.broadcasted_iota(jnp.int32, (groups, rows), 1) // period
        == lax.broadcasted_iota(jnp.int32, (groups, rows), 0)
    ).astype(BF16)

    def pick(i):
        copies[i].wait()
        kept = buf[i].reshape(groups, period, width) * keep[None]
        return jnp.dot(member, kept.reshape(rows, width), preferred_element_type=F32)

    q, k, v = pick(0), pick(1), pick(2)
    low = lane_is_low((groups, 128))
    low_half = lane_is_low((groups // 2, 128))
    for pair in range(HEADS // 2):
        lanes = slice(pair * 128, pair * 128 + 128)
        qb, kb, vb = q[:, lanes], k[:, lanes], v[:, lanes]
        top, bottom = vb[: groups // 2], vb[groups // 2 :]
        even, odd = slot_of(2 * pair, n_row, period), slot_of(2 * pair + 1, n_row, period)
        x_ref[even, :groups] = jnp.where(low, qb, swap(kb)).astype(BF16)
        x_ref[even, groups:] = jnp.where(low_half, top, swap(bottom)).astype(BF16)
        x_ref[odd, :groups] = jnp.where(low, swap(qb), kb).astype(BF16)
        x_ref[odd, groups:] = jnp.where(low_half, swap(top), bottom).astype(BF16)
    for rest in range(HEADS, x_ref.shape[0]):
        x_ref[slot_of(rest, n_row, period)] = jnp.zeros(x_ref.shape[1:], BF16)


def middle_kernel(y_ref, z_ref):
    y = y_ref[...].astype(F32)
    first, second, val = y[:, 0, :], y[:, 16, :], y[:, 32, :]
    low = lane_is_low(first.shape)
    top = jnp.where(low, swap(first), swap(val)).astype(BF16)
    bottom = jnp.where(low, swap(second), val).astype(BF16)
    both = jnp.concatenate([top, bottom], axis=0)
    for i in range(z_ref.shape[0]):
        z_ref[i] = both


def soft(scores):
    top = jnp.max(scores, axis=-1, keepdims=True)
    weights = jnp.exp((scores - top) * 0.125)
    total = jnp.sum(weights, axis=-1, keepdims=True)
    return weights.astype(BF16), total, top * 0.125 + jnp.log(total)


def merge(out_a, lse_a, out_b, lse_b):
    top = jnp.maximum(lse_a, lse_b)
    wa, wb = jnp.exp(lse_a - top), jnp.exp(lse_b - top)
    total = wa + wb
    return (wa * out_a + wb * out_b) / total, top + jnp.log(total)


def segment_kernel(y_ref, out_ref):
    n, _, _ = y_ref.shape
    qk = y_ref[:, :32, :].reshape(n * 32, 128).astype(F32)
    low = lane_is_low(qk.shape)
    query = jnp.where(low, qk, 0.0).astype(BF16)
    key = swap(qk).astype(BF16)
    val = y_ref[:, 32:, :].astype(F32).reshape(n * 16, 128)
    other = swap(val).reshape(n, 16, 128)
    val = jnp.concatenate([val.reshape(n, 16, 128), other], axis=1).reshape(n * 32, 128).astype(BF16)
    scores = lax.dot_general(query, key, NT, preferred_element_type=F32)
    probs, total, lse = soft(scores)
    out = jnp.dot(probs, val, preferred_element_type=F32) / total
    out_ref[...] = jnp.where(low, out, lse).reshape(n, 32, 128)


def sequence_kernel(y_ref, z_ref, o_ref, ret_ref):
    n = y_ref.shape[0]
    q2 = jnp.concatenate([y_ref[:, 16 * i : 16 * i + 16, :].astype(F32)[:, 0, :] for i in range(2)], axis=0)
    q2 = jnp.where(lane_is_low(q2.shape), q2, 0.0).astype(BF16)
    kv = z_ref[...].reshape(-1, 128)
    scores = lax.dot_general(q2, kv, NT, preferred_element_type=F32)
    probs, total, lse = soft(scores)
    out = swap(jnp.dot(probs, kv, preferred_element_type=F32) / total)
    row = lax.broadcasted_iota(jnp.int32, (n, 16, 128), 1)
    halves = []
    for i in range(2):
        old = o_ref[:, 16 * i : 16 * i + 16, :]
        first = old[:, 0, :]
        part = slice(n * i, n * i + n)
        mixed, lse_new = merge(first, swap(first), out[part], lse[part])
        first = jnp.where(lane_is_low(first.shape), mixed, swap(lse_new))
        halves.append(jnp.where(row == 0, first[:, None, :], old))
    low, high = halves
    ret_ref[:, :16, :] = jnp.where(lane_is_low(low.shape), low, swap(high))
    quarter = lax.broadcasted_iota(jnp.int32, (n, 8, 128), 2) // 32
    ret_ref[:, 16:, :] = jnp.where(
        quarter < 2,
        jnp.where(quarter == 0, low[:, :8, 64:65], low[:, 8:, 64:65]),
        jnp.where(quarter == 2, high[:, :8, 64:65], high[:, 8:, 64:65]),
    )


def split(x):
    def leading(y):
        scaled = y * 65537.0
        return scaled - (scaled - y)

    high = leading(x)
    rest = x - high
    mid = leading(rest)
    return high, mid, rest - mid


def local_kernel(start, q_hbm, k_hbm, v_hbm, *rest):
    o_ref, buf, sem, out_scr, lse_scr = rest[-5:]
    step, steps = pl.program_id(0), pl.num_programs(0)
    rows = q_hbm.shape[0]
    groups = rows // 16

    def copies(pair):
        lanes, slot = pl.ds(pl.multiple_of((start + pair) * 128, 128), 128), lax.rem(pair, 2)
        return [
            pltpu.make_async_copy(hbm.at[:, lanes], buf.at[slot, i], sem.at[slot, i])
            for i, hbm in enumerate((q_hbm, k_hbm, v_hbm))
        ]

    @pl.when(step == 0)
    def _():
        for copy in copies(step):
            copy.start()

    @pl.when(step + 1 < steps)
    def _():
        for copy in copies(step + 1):
            copy.start()

    for copy in copies(step):
        copy.wait()
    slot = lax.rem(step, 2)
    q, k, v = buf[slot, 0], buf[slot, 1], buf[slot, 2]
    low = lane_is_low(q.shape)
    outs, lses = [], []
    for half in range(2):
        query = jnp.where(low == (half == 0), q, jnp.zeros_like(q))
        scores = lax.dot_general(query, k, NT, preferred_element_type=F32)
        probs, total, lse = soft(scores)
        outs.append(jnp.dot(probs, v, preferred_element_type=F32) / total)
        lses.append(lse)
    out = jnp.where(low, outs[0], outs[1])
    out_scr[...] = out
    lse_scr[...] = jnp.where(low, lses[0], lses[1])
    o_ref[:rows, :] = out.astype(BF16)
    lowr = lane_is_low((groups, 128))
    even = pl.ds(2 * (start + step), groups, stride=16)
    odd = pl.ds(2 * (start + step) + 1, groups, stride=16)
    at = rows
    for scr in (out_scr, lse_scr):
        for piece in split(jnp.where(lowr, scr[even, :], scr[odd, :])):
            o_ref[at : at + groups, :] = piece.astype(BF16)
            at += groups


def finish_kernel(period, n_row, local, r_ref, w_ref, out_hbm, buf, out_sem):
    rows, width = out_hbm.shape
    groups = rows // period
    n = r_ref.shape[0]
    low = lane_is_low((groups, 128))
    remote = []
    for pair in range(HEADS // 2):
        back = [r_ref[slot_of(2 * pair + half, n_row, n)] for half in range(2)]
        outs = [b[: groups // 2] for b in back]
        lses = [b[groups // 2 :] for b in back]
        lse = [
            jnp.concatenate([b[:, 32 * i : 32 * i + 1] for i in range(4)], axis=0) for b in lses
        ]
        low_half = lane_is_low(outs[0].shape)
        out_b = jnp.concatenate(
            [jnp.where(low_half, outs[0], swap(outs[1])), jnp.where(low_half, swap(outs[0]), outs[1])], axis=0
        )
        remote.append((out_b, jnp.where(low, lse[0], lse[1])))
    blocks = []
    for pair in range(HEADS // 2):
        lanes = slice(pair * 128, pair * 128 + 128)
        pieces = [
            local[rows + i * groups : rows + (i + 1) * groups, lanes].astype(F32) for i in range(6)
        ]
        out_a, lse_a = (pieces[i] + pieces[i + 1] + pieces[i + 2] for i in (0, 3))
        blocks.append(merge(out_a, lse_a, *remote[pair])[0])
    merged = jnp.concatenate(blocks, axis=1)
    keep = chosen_lanes(period, width)[None]
    own = local[:rows, :].astype(F32).reshape(groups, period, width)
    mixed = jnp.where(keep, merged[:, None, :], own).reshape(rows, width).astype(BF16)
    chunks = buf.shape[0]
    wide = width // chunks
    copies = []
    for c in range(chunks):
        part = pl.ds(c * wide, wide)
        buf[c] = jnp.dot(mixed, w_ref[:, part], preferred_element_type=F32).astype(BF16)
        copy = pltpu.make_async_copy(buf.at[c], out_hbm.at[:, part], out_sem.at[c])
        copy.start()
        copies.append(copy)
    for copy in copies:
        copy.wait()


def shards(queries, keys, values, out_weight):
    n_row, n_col = lax.axis_size("row"), lax.axis_size("col")
    rows, width = queries.shape
    groups = rows // n_col
    shape = jax.ShapeDtypeStruct

    def call(kernel, out, mib=16, **kw):
        params = pltpu.CompilerParams(vmem_limit_bytes=mib * 1024 * 1024)
        return pl.pallas_call(kernel, out_shape=out, compiler_params=params, **kw)

    anywhere = pl.BlockSpec(memory_space=pl.ANY)
    distant = pl.BlockSpec(memory_space=pltpu.HBM)
    whole = pl.BlockSpec(memory_space=pltpu.VMEM)
    packed = call(
        lambda *refs: pack_kernel(n_col, n_row, *refs),
        shape((n_col, groups * 3 // 2, 128), BF16),
        mib=56,
        in_specs=[distant] * 3,
        scratch_shapes=[pltpu.VMEM((3, rows, width), BF16), pltpu.SemaphoreType.DMA((3,))],
    )(queries, keys, values)
    def local(start, count, inputs, aliases):
        pairs = rows * rows * 2 * count
        return call(
            lambda *refs: local_kernel(start, *refs),
            shape((rows + 6 * groups, width), BF16),
            mib=54,
            grid=(count,),
            in_specs=[distant] * 3 + [anywhere] * (len(inputs) - 3),
            out_specs=pl.BlockSpec((rows + 6 * groups, 128), lambda i: (0, start + i)),
            scratch_shapes=[
                pltpu.VMEM((2, 3, rows, 128), BF16),
                pltpu.SemaphoreType.DMA((2, 3)),
                pltpu.VMEM((rows, 128), F32),
                pltpu.VMEM((rows, 128), F32),
            ],
            input_output_aliases=aliases,
            cost_estimate=pl.CostEstimate(
                flops=pairs * 1024, bytes_accessed=count * rows * 128 * 10, transcendentals=pairs
            ),
        )(*inputs)

    inputs = (queries, keys, values)
    packed, *inputs = lax.optimization_barrier((packed, *inputs))
    mine = lax.all_to_all(packed, "col", 0, 0)
    early = HEADS // 4
    first = local(0, early, inputs, {})
    mine, first = lax.optimization_barrier((mine, first))
    top_own = call(middle_kernel, shape((n_row, 2 * n_col, 128), BF16))(mine)
    top_own, mine, first, *inputs = lax.optimization_barrier((top_own, mine, first, *inputs))
    owners = [
        [r * n_col + (c + 2 * r // n_row * (n_col // 2)) % n_col for r in range(n_row)]
        for c in range(n_col)
    ]
    top_all = lax.all_to_all(top_own, ("row", "col"), 0, 0, axis_index_groups=owners)
    second = local(early, HEADS // 2 - early, (*inputs, first), {3: 0})
    mine, second = lax.optimization_barrier((mine, second))
    segment = call(segment_kernel, shape((n_col, groups, 128), F32))(mine)
    top_all, segment = lax.optimization_barrier((top_all, segment))
    ret = call(
        sequence_kernel,
        shape((n_col, groups * 3 // 4, 128), F32),
        cost_estimate=pl.CostEstimate(flops=10**10, bytes_accessed=10**6, transcendentals=0),
    )(mine, top_all, segment)
    back = lax.all_to_all(ret, "col", 0, 0)
    return call(
        lambda *refs: finish_kernel(n_col, n_row, *refs),
        shape((rows, width), BF16),
        in_specs=[whole] * 3,
        out_specs=anywhere,
        scratch_shapes=[pltpu.VMEM((3, rows, width // 3), BF16), pltpu.SemaphoreType.DMA((3,))],
    )(second, back, out_weight)


def solution(mesh):
    placed = (P(("row", "col"), None), P(("row", "col"), None), P(("row", "col"), None), P())
    return jax.shard_map(
        shards, mesh=mesh, in_specs=placed, out_specs=P(("row", "col"), None), check_vma=False
    )
```

time: 63.3 us -> 54.3 us (0.86)
  blocking collectives: 37.8 us -> 13.3 us
  starting transfers between devices: 4.2 us -> 17.9 us
  local copies, waits for them, and re-layouts: 7.03 us -> 0.01 us
  waiting for transfers between devices: 0.72 us -> 5.37 us
  Pallas kernels: 13 us -> 17.2 us
    all_to_all x2 -> x1, blocking collectives: 37.8 us -> 13.3 us  [shards(): back = lax.all_to_all(ret, 'col', 0, 0)]
    all_to_all x1 -> x2, starting transfers between devices: 4.2 us -> 17.9 us  [the longest x1 9.2 us: shards(): mine = lax.all_to_all(packed, 'col', 0, 0)]
    unnamed x22 -> x4, local copies, waits for them, and re-layouts: 7.03 us -> 0.01 us
    all_to_all x1 -> x2, waiting for transfers between devices: 0.72 us -> 5.37 us  [the longest x1 3.17 us: shards(): mine = lax.all_to_all(packed, 'col', 0, 0)]
    pallas_call x4 -> x6, Pallas kernels: 12.9 us -> 16.5 us  [the longest x2 10.5 us: local(): call(lambda *refs: local_kernel(start, *refs), shape((rows + 6 * groups,...]
    pallas_call x1, Pallas kernels: 0.1 us -> 0.75 us  [shards(): top_own = call(middle_kernel, shape((n_row, 2 * n_col, 128), BF16))(mine)]
  transfers between devices with their start and end apart: 1 -> 2, of which waited for: 1 -> 2; matrix products, arithmetic and copies ran while one was open for 0% -> 0% of each run, Pallas kernels for 12% -> 21%
where the time goes in v2:
time: 54.3 us; the launch traced here: 53.9 us
  starting transfers between devices  17.9 us (33%)
  Pallas kernels  17.2 us (32%)
  blocking collectives  13.3 us (24%)
  waiting for transfers between devices  5.37 us (10%)
    all_to_all x1, blocking collectives, shards(): back = lax.all_to_all(ret, 'col', 0, 0)  13.3 us
    pallas_call x2, Pallas kernels, local(): call(lambda *refs: local_kernel(start, *refs), shape((rows + 6 * groups,...  10.5 us
    all_to_all x1, starting transfers between devices, shards(): mine = lax.all_to_all(packed, 'col', 0, 0)  9.2 us
    all_to_all x1, starting transfers between devices, shards(): lax.all_to_all(top_own, ('row', 'col'), 0, 0, axis_index_groups=owners)  8.75 us
    all_to_all x1, waiting for transfers between devices, shards(): mine = lax.all_to_all(packed, 'col', 0, 0)  3.17 us
    pallas_call x1, Pallas kernels, shards(): call(lambda *refs: pack_kernel(n_col, n_row, *refs), shape((n_col, groups...  2.71 us
    all_to_all x1, waiting for transfers between devices, shards(): lax.all_to_all(top_own, ('row', 'col'), 0, 0, axis_index_groups=owners)  2.2 us
    pallas_call x1, Pallas kernels, shards(): call(lambda *refs: finish_kernel(n_col, n_row, *refs), shape((rows, width...  1.79 us
  transfers between devices with their start and end apart: 2, of which 2 were waited for; matrix products, arithmetic and copies ran while one was open for 0% of the time, Pallas kernels for 21%

profile of v2, /device:TPU:1, one launch (start us, length us, event | category | flops | bytes accessed | tf_op | source)
XLA Modules:
  0.0 53.9 jit_solution(6296716054711688081)
XLA Ops:
  0.0 2.7 %shard_map.46 = bf16[16,48,128]{2,1,0:T(8,128)(2,1)} custom-call(bf16[512,768]{1,0:T(8,128)(2,1)} %refs_0_.3, bf16[512,768]{1,0:T(8,128)(2,1)} %refs_1_.3, bf16[512,768]{1,0:T(8,128)(2,1)} %refs_2_.4), custom_call_target="tpu_custom_call" | custom-call | tf_op jit(solution)/shard_map/pallas_call | solution.py:252
  2.7 9.2 %all-to-all-start = ((bf16[16,48,128]{2,1,0:T(8,128)(2,1)}), bf16[16,48,128]{2,1,0:T(8,128)(2,1)S(1)}, u32[]{:S(2)}, u32[]{:S(2)}) async-start(bf16[16,48,128]{2,1,0:T(8,128)(2,1)} %shard_map.46), calls=%async_computation | async-start | bytes 393216 | tf_op jit(solution)/shard_map/all_to_all | solution.py:282
  11.9 5.2 %shard_map.47.refs_3_ = bf16[704,768]{1,0:T(8,128)(2,1)} custom-call(bf16[512,768]{1,0:T(8,128)(2,1)} %refs_0_.3, bf16[512,768]{1,0:T(8,128)(2,1)} %refs_1_.3, bf16[512,768]{1,0:T(8,128)(2,1)} %refs_2_.4), custom_call_target="tpu_custom_call" | custom-call | flops 1610612736 | bytes 1966080 | tf_op jit(solution)/shard_map/pallas_call | solution.py:261
  17.2 3.2 %all-to-all-done.y_ref = bf16[16,48,128]{2,1,0:T(8,128)(2,1)S(1)} async-done(((bf16[16,48,128]{2,1,0:T(8,128)(2,1)}), bf16[16,48,128]{2,1,0:T(8,128)(2,1)S(1)}, u32[]{:S(2)}, u32[]{:S(2)}) %all-to-all-start) | async-done | bytes 196640 | tf_op jit(solution)/shard_map/all_to_all | solution.py:282
  20.3 0.8 %shard_map.48 = bf16[16,32,128]{2,1,0:T(8,128)(2,1)} custom-call(bf16[16,48,128]{2,1,0:T(8,128)(2,1)S(1)} %all-to-all-done.y_ref), custom_call_target="tpu_custom_call" | custom-call | tf_op jit(solution)/shard_map/pallas_call | solution.py:286
  21.1 8.7 %all-to-all-start.1 = ((bf16[16,32,128]{2,1,0:T(8,128)(2,1)}), bf16[16,32,128]{2,1,0:T(8,128)(2,1)S(1)}, u32[]{:S(2)}, u32[]{:S(2)}) async-start(bf16[16,32,128]{2,1,0:T(8,128)(2,1)} %shard_map.48), calls=%async_computation.1 | async-start | bytes 262144 | tf_op jit(solution)/shard_map/all_to_all | solution.py:292
  29.8 5.3 %shard_map.49.refs_0_ = bf16[704,768]{1,0:T(8,128)(2,1)} custom-call(bf16[512,768]{1,0:T(8,128)(2,1)} %refs_0_.3, bf16[512,768]{1,0:T(8,128)(2,1)} %refs_1_.3, bf16[512,768]{1,0:T(8,128)(2,1)} %refs_2_.4, bf16[704,768]{1,0:T(8,128)(2,1)} %shard_map.47.refs_3_), custom_call_target="tpu_custom_call", output_to_operand_aliasing={{}: (3, {})} | custom-call | flops 1610612736 | bytes 1966080 | tf_op jit(solution)/shard_map/pallas_call | solution.py:261
  35.1 0.9 %shard_map.50.o_ref = f32[16,32,128]{2,1,0:T(8,128)S(1)} custom-call(bf16[16,48,128]{2,1,0:T(8,128)(2,1)S(1)} %all-to-all-done.y_ref), custom_call_target="tpu_custom_call" | custom-call | tf_op jit(solution)/shard_map/pallas_call | solution.py:295
  36.0 2.2 %all-to-all-done.1.z_ref = bf16[16,32,128]{2,1,0:T(8,128)(2,1)S(1)} async-done(((bf16[16,32,128]{2,1,0:T(8,128)(2,1)}), bf16[16,32,128]{2,1,0:T(8,128)(2,1)S(1)}, u32[]{:S(2)}, u32[]{:S(2)}) %all-to-all-start.1) | async-done | bytes 131104 | tf_op jit(solution)/shard_map/all_to_all | solution.py:292
  38.2 0.0 copy-start
  38.2 0.0 copy-start.1
  38.2 0.6 %shard_map.51 = f32[16,24,128]{2,1,0:T(8,128)S(1)} custom-call(bf16[16,48,128]{2,1,0:T(8,128)(2,1)S(1)} %all-to-all-done.y_ref, bf16[16,32,128]{2,1,0:T(8,128)(2,1)S(1)} %all-to-all-done.1.z_ref, f32[16,32,128]{2,1,0:T(8,128)S(1)} %shard_map.50.o_ref), custom_call_target="tpu_custom_call" | custom-call | flops 10000000000 | bytes 1000000 | tf_op jit(solution)/shard_map/pallas_call | solution.py:297
  38.8 13.3 %all_to_all.15.refs_1_ = f32[16,24,128]{2,1,0:T(8,128)S(1)} all-to-all(f32[16,24,128]{2,1,0:T(8,128)S(1)} %shard_map.51), channel_id=1, replica_groups=mesh['row'=16,'col'=16] {'col'}, dimensions={0} | all-to-all | bytes 393216 | tf_op jit(solution)/shard_map/all_to_all | solution.py:302
  52.2 0.0 copy-done
  52.2 0.0 copy-done.1
  52.2 1.8 %shard_map.52 = bf16[512,768]{1,0:T(8,128)(2,1)} custom-call(bf16[704,768]{1,0:T(8,128)(2,1)S(1)} %copy-done.1, f32[16,24,128]{2,1,0:T(8,128)S(1)} %all_to_all.15.refs_1_, bf16[768,768]{1,0:T(8,128)(2,1)S(1)} %copy-done), custom_call_target="tpu_custom_call" | custom-call | tf_op jit(solution)/shard_map/pallas_call | solution.py:303
Async XLA Ops:
  2.7 17.6 %all-to-all-start = ((bf16[16,48,128]{2,1,0:T(8,128)(2,1)}), bf16[16,48,128]{2,1,0:T(8,128)(2,1)S(1)}, u32[]{:S(2)}, u32[]{:S(2)}) async-start(bf16[16,48,128]{2,1,0:T(8,128)(2,1)} %shard_map.46), calls=%async_computation | async-start | bytes 393216 | tf_op jit(solution)/shard_map/all_to_all | solution.py:282
  21.1 17.1 %all-to-all-start.1 = ((bf16[16,32,128]{2,1,0:T(8,128)(2,1)}), bf16[16,32,128]{2,1,0:T(8,128)(2,1)S(1)}, u32[]{:S(2)}, u32[]{:S(2)}) async-start(bf16[16,32,128]{2,1,0:T(8,128)(2,1)} %shard_map.48), calls=%async_computation.1 | async-start | bytes 262144 | tf_op jit(solution)/shard_map/all_to_all | solution.py:292
  38.2 14.0 %copy-start = (bf16[768,768]{1,0:T(8,128)(2,1)S(1)}, bf16[768,768]{1,0:T(8,128)(2,1)}, u32[]{:S(2)}) copy-start(bf16[768,768]{1,0:T(8,128)(2,1)} %refs_2_.5) | copy-start | bytes 3538948
  38.2 14.0 %copy-start.1 = (bf16[704,768]{1,0:T(8,128)(2,1)S(1)}, bf16[704,768]{1,0:T(8,128)(2,1)}, u32[]{:S(2)}) copy-start(bf16[704,768]{1,0:T(8,128)(2,1)} %shard_map.49.refs_0_) | copy-start | bytes 3244036

commit v3 on v2

--- a/solution.py
+++ b/solution.py
@@ -6,6 +6,8 @@
 from jax.sharding import PartitionSpec as P
 
 HEADS = 12
+LOG2E = 1.4426950408889634
+LSE_LANE = 125
 F32 = jnp.float32
 BF16 = jnp.bfloat16
 NT = (((1,), (1,)), ((), ()))
@@ -26,8 +28,10 @@
 
 
 def slot_of(head, n_row, n_col):
-    moved = lax.div(lax.axis_index("row"), n_row // 2) * (n_col // 2)
-    return lax.rem(head + moved, n_col)
+    side = int(n_col**0.5)
+    upper = lax.div(lax.axis_index("row"), n_row // 2)
+    z = head // side
+    return (z + upper * (side - 1 - 2 * z)) * side + head % side
 
 
 def pack_kernel(period, n_row, q_hbm, k_hbm, v_hbm, x_ref, buf, sem):
@@ -50,17 +54,21 @@
         kept = buf[i].reshape(groups, period, width) * keep[None]
         return jnp.dot(member, kept.reshape(rows, width), preferred_element_type=F32)
 
-    q, k, v = pick(0), pick(1), pick(2)
+    q, k = pick(0), pick(1)
     low = lane_is_low((groups, 128))
     low_half = lane_is_low((groups // 2, 128))
-    for pair in range(HEADS // 2):
-        lanes = slice(pair * 128, pair * 128 + 128)
-        qb, kb, vb = q[:, lanes], k[:, lanes], v[:, lanes]
-        top, bottom = vb[: groups // 2], vb[groups // 2 :]
-        even, odd = slot_of(2 * pair, n_row, period), slot_of(2 * pair + 1, n_row, period)
+    pairs = [
+        (slice(i * 128, i * 128 + 128), slot_of(2 * i, n_row, period), slot_of(2 * i + 1, n_row, period))
+        for i in range(HEADS // 2)
+    ]
+    for lanes, even, odd in pairs:
+        qb, kb = q[:, lanes], k[:, lanes]
         x_ref[even, :groups] = jnp.where(low, qb, swap(kb)).astype(BF16)
+        x_ref[odd, :groups] = jnp.where(low, swap(qb), kb).astype(BF16)
+    v = pick(2)
+    for lanes, even, odd in pairs:
+        top, bottom = v[: groups // 2, lanes], v[groups // 2 :, lanes]
         x_ref[even, groups:] = jnp.where(low_half, top, swap(bottom)).astype(BF16)
-        x_ref[odd, :groups] = jnp.where(low, swap(qb), kb).astype(BF16)
         x_ref[odd, groups:] = jnp.where(low_half, swap(top), bottom).astype(BF16)
     for rest in range(HEADS, x_ref.shape[0]):
         x_ref[slot_of(rest, n_row, period)] = jnp.zeros(x_ref.shape[1:], BF16)
@@ -79,7 +87,7 @@
 
 def soft(scores):
     top = jnp.max(scores, axis=-1, keepdims=True)
-    weights = jnp.exp((scores - top) * 0.125)
+    weights = jnp.exp2((scores - top) * (0.125 * LOG2E))
     total = jnp.sum(weights, axis=-1, keepdims=True)
     return weights.astype(BF16), total, top * 0.125 + jnp.log(total)
 
@@ -123,14 +131,12 @@
         mixed, lse_new = merge(first, swap(first), out[part], lse[part])
         first = jnp.where(lane_is_low(first.shape), mixed, swap(lse_new))
         halves.append(jnp.where(row == 0, first[:, None, :], old))
-    low, high = halves
-    ret_ref[:, :16, :] = jnp.where(lane_is_low(low.shape), low, swap(high))
-    quarter = lax.broadcasted_iota(jnp.int32, (n, 8, 128), 2) // 32
-    ret_ref[:, 16:, :] = jnp.where(
-        quarter < 2,
-        jnp.where(quarter == 0, low[:, :8, 64:65], low[:, 8:, 64:65]),
-        jnp.where(quarter == 2, high[:, :8, 64:65], high[:, 8:, 64:65]),
-    )
+    block = jnp.concatenate(halves, axis=1)
+    high, mid, tail = split(block)
+    lane = lax.broadcasted_iota(jnp.int32, block.shape, 2)
+    last = jnp.where(lane == LSE_LANE, high, jnp.where(lane == LSE_LANE + 1, mid, tail))
+    send = jnp.where(lane < 64, high, jnp.where(lane < LSE_LANE, swap(mid), last))
+    ret_ref[...] = send.astype(BF16)
 
 
 def split(x):
@@ -170,19 +176,26 @@
     for copy in copies(step):
         copy.wait()
     slot = lax.rem(step, 2)
-    q, k, v = buf[slot, 0], buf[slot, 1], buf[slot, 2]
-    low = lane_is_low(q.shape)
-    outs, lses = [], []
-    for half in range(2):
-        query = jnp.where(low == (half == 0), q, jnp.zeros_like(q))
-        scores = lax.dot_general(query, k, NT, preferred_element_type=F32)
-        probs, total, lse = soft(scores)
-        outs.append(jnp.dot(probs, v, preferred_element_type=F32) / total)
-        lses.append(lse)
-    out = jnp.where(low, outs[0], outs[1])
-    out_scr[...] = out
-    lse_scr[...] = jnp.where(low, lses[0], lses[1])
-    o_ref[:rows, :] = out.astype(BF16)
+    k, v = buf[slot, 1], buf[slot, 2]
+    tall = rows // 2
+    low = lane_is_low((tall, 128))
+    parts = [slice(i * tall, i * tall + tall) for i in range(2)]
+    scores = {}
+    for i, part in enumerate(parts):
+        q = buf[slot, 0, part, :]
+        for half in range(2):
+            query = jnp.where(low == (half == 0), q, jnp.zeros_like(q))
+            scores[i, half] = lax.dot_general(query, k, NT, preferred_element_type=F32)
+    for i, part in enumerate(parts):
+        outs, lses = [], []
+        for half in range(2):
+            probs, total, lse = soft(scores[i, half])
+            outs.append(jnp.dot(probs, v, preferred_element_type=F32) / total)
+            lses.append(lse)
+        out = jnp.where(low, outs[0], outs[1])
+        out_scr[part, :] = out
+        lse_scr[part, :] = jnp.where(low, lses[0], lses[1])
+        o_ref[part, :] = out.astype(BF16)
     lowr = lane_is_low((groups, 128))
     even = pl.ds(2 * (start + step), groups, stride=16)
     odd = pl.ds(2 * (start + step) + 1, groups, stride=16)
@@ -198,19 +211,19 @@
     groups = rows // period
     n = r_ref.shape[0]
     low = lane_is_low((groups, 128))
+    backs = [r_ref[slot_of(head, n_row, n)] for head in range(HEADS)]
+    source = lax.broadcasted_iota(jnp.int32, (128, 128), 0)
+    lse_all = jnp.dot(
+        jnp.concatenate(backs, axis=0), (source >= LSE_LANE).astype(BF16), preferred_element_type=F32
+    )
+    has_low = lax.broadcasted_iota(jnp.int32, (groups, 128), 1) < LSE_LANE - 64
     remote = []
     for pair in range(HEADS // 2):
-        back = [r_ref[slot_of(2 * pair + half, n_row, n)] for half in range(2)]
-        outs = [b[: groups // 2] for b in back]
-        lses = [b[groups // 2 :] for b in back]
-        lse = [
-            jnp.concatenate([b[:, 32 * i : 32 * i + 1] for i in range(4)], axis=0) for b in lses
-        ]
-        low_half = lane_is_low(outs[0].shape)
-        out_b = jnp.concatenate(
-            [jnp.where(low_half, outs[0], swap(outs[1])), jnp.where(low_half, swap(outs[0]), outs[1])], axis=0
-        )
-        remote.append((out_b, jnp.where(low, lse[0], lse[1])))
+        outs = [backs[2 * pair + half].astype(F32) for half in range(2)]
+        outs = [o + jnp.where(has_low, swap(o), 0.0) for o in outs]
+        at = 2 * pair * groups
+        lse = [lse_all[at + half * groups : at + (half + 1) * groups] for half in range(2)]
+        remote.append((jnp.where(low, outs[0], swap(outs[1])), jnp.where(low, lse[0], lse[1])))
     blocks = []
     for pair in range(HEADS // 2):
         lanes = slice(pair * 128, pair * 128 + 128)
@@ -280,13 +293,14 @@
     inputs = (queries, keys, values)
     packed, *inputs = lax.optimization_barrier((packed, *inputs))
     mine = lax.all_to_all(packed, "col", 0, 0)
-    early = HEADS // 4
+    early = HEADS // 3
     first = local(0, early, inputs, {})
     mine, first = lax.optimization_barrier((mine, first))
     top_own = call(middle_kernel, shape((n_row, 2 * n_col, 128), BF16))(mine)
     top_own, mine, first, *inputs = lax.optimization_barrier((top_own, mine, first, *inputs))
+    side = int(n_col**0.5)
     owners = [
-        [r * n_col + (c + 2 * r // n_row * (n_col // 2)) % n_col for r in range(n_row)]
+        [r * n_col + (c if 2 * r < n_row else (side - 1 - c // side) * side + c % side) for r in range(n_row)]
         for c in range(n_col)
     ]
     top_all = lax.all_to_all(top_own, ("row", "col"), 0, 0, axis_index_groups=owners)
@@ -296,7 +310,7 @@
     top_all, segment = lax.optimization_barrier((top_all, segment))
     ret = call(
         sequence_kernel,
-        shape((n_col, groups * 3 // 4, 128), F32),
+        shape((n_col, groups, 128), BF16),
         cost_estimate=pl.CostEstimate(flops=10**10, bytes_accessed=10**6, transcendentals=0),
     )(mine, top_all, segment)
     back = lax.all_to_all(ret, "col", 0, 0)

time: 54.3 us -> 53.5 us (0.985)
  Pallas kernels: 17.2 us -> 16.2 us
  blocking collectives: 13.3 us -> 14.1 us
    pallas_call x2, Pallas kernels: 10.5 us -> 9.44 us  [local(): call(lambda *refs: local_kernel(start, *refs), shape((rows + 6 * groups,...]
    all_to_all x1, blocking collectives: 13.3 us -> 14.1 us  [shards(): back = lax.all_to_all(ret, 'col', 0, 0)]
    all_to_all x1, starting transfers between devices: 8.75 us -> 8.19 us  [shards(): lax.all_to_all(top_own, ('row', 'col'), 0, 0, axis_index_groups=owners)]
    all_to_all x1, waiting for transfers between devices: 2.2 us -> 2.75 us  [shards(): lax.all_to_all(top_own, ('row', 'col'), 0, 0, axis_index_groups=owners)]
  transfers between devices with their start and end apart: 2 -> 2, of which waited for: 2 -> 2; matrix products, arithmetic and copies ran while one was open for 0% -> 0% of each run, Pallas kernels for 21% -> 19%
where the time goes in v3:
time: 53.5 us; the launch traced here: 53.1 us
  starting transfers between devices  17.4 us (33%)
  Pallas kernels  16.2 us (30%)
  blocking collectives  14.1 us (26%)
  waiting for transfers between devices  5.43 us (10%)
    all_to_all x1, blocking collectives, shards(): back = lax.all_to_all(ret, 'col', 0, 0)  14.1 us
    pallas_call x2, Pallas kernels, local(): call(lambda *refs: local_kernel(start, *refs), shape((rows + 6 * groups,...  9.44 us
    all_to_all x1, starting transfers between devices, shards(): mine = lax.all_to_all(packed, 'col', 0, 0)  9.2 us
    all_to_all x1, starting transfers between devices, shards(): lax.all_to_all(top_own, ('row', 'col'), 0, 0, axis_index_groups=owners)  8.19 us
    pallas_call x1, Pallas kernels, shards(): call(lambda *refs: pack_kernel(n_col, n_row, *refs), shape((n_col, groups...  2.8 us
    all_to_all x1, waiting for transfers between devices, shards(): lax.all_to_all(top_own, ('row', 'col'), 0, 0, axis_index_groups=owners)  2.75 us
    all_to_all x1, waiting for transfers between devices, shards(): mine = lax.all_to_all(packed, 'col', 0, 0)  2.67 us
    pallas_call x1, Pallas kernels, shards(): call(lambda *refs: finish_kernel(n_col, n_row, *refs), shape((rows, width...  1.77 us
  transfers between devices with their start and end apart: 2, of which 2 were waited for; matrix products, arithmetic and copies ran while one was open for 0% of the time, Pallas kernels for 19%

profile of v3, /device:TPU:1, one launch (start us, length us, event | category | flops | bytes accessed | tf_op | source)
XLA Modules:
  0.0 53.1 jit_solution(17462369801714770858)
XLA Ops:
  0.0 2.8 %shard_map.46 = bf16[16,48,128]{2,1,0:T(8,128)(2,1)} custom-call(bf16[512,768]{1,0:T(8,128)(2,1)} %refs_0_.3, bf16[512,768]{1,0:T(8,128)(2,1)} %refs_1_.3, bf16[512,768]{1,0:T(8,128)(2,1)} %refs_2_.4), custom_call_target="tpu_custom_call" | custom-call | tf_op jit(solution)/shard_map/pallas_call | solution.py:265
  2.8 9.2 %all-to-all-start = ((bf16[16,48,128]{2,1,0:T(8,128)(2,1)}), bf16[16,48,128]{2,1,0:T(8,128)(2,1)S(1)}, u32[]{:S(2)}, u32[]{:S(2)}) async-start(bf16[16,48,128]{2,1,0:T(8,128)(2,1)} %shard_map.46), calls=%async_computation | async-start | bytes 393216 | tf_op jit(solution)/shard_map/all_to_all | solution.py:295
  12.0 5.7 %shard_map.47.refs_3_ = bf16[704,768]{1,0:T(8,128)(2,1)} custom-call(bf16[512,768]{1,0:T(8,128)(2,1)} %refs_0_.3, bf16[512,768]{1,0:T(8,128)(2,1)} %refs_1_.3, bf16[512,768]{1,0:T(8,128)(2,1)} %refs_2_.4), custom_call_target="tpu_custom_call" | custom-call | flops 2147483648 | bytes 2621440 | tf_op jit(solution)/shard_map/pallas_call | solution.py:274
  17.8 2.7 %all-to-all-done.y_ref = bf16[16,48,128]{2,1,0:T(8,128)(2,1)S(1)} async-done(((bf16[16,48,128]{2,1,0:T(8,128)(2,1)}), bf16[16,48,128]{2,1,0:T(8,128)(2,1)S(1)}, u32[]{:S(2)}, u32[]{:S(2)}) %all-to-all-start) | async-done | bytes 196640 | tf_op jit(solution)/shard_map/all_to_all | solution.py:295
  20.4 0.8 %shard_map.48 = bf16[16,32,128]{2,1,0:T(8,128)(2,1)} custom-call(bf16[16,48,128]{2,1,0:T(8,128)(2,1)S(1)} %all-to-all-done.y_ref), custom_call_target="tpu_custom_call" | custom-call | tf_op jit(solution)/shard_map/pallas_call | solution.py:299
  21.2 8.2 %all-to-all-start.1 = ((bf16[16,32,128]{2,1,0:T(8,128)(2,1)}), bf16[16,32,128]{2,1,0:T(8,128)(2,1)S(1)}, u32[]{:S(2)}, u32[]{:S(2)}) async-start(bf16[16,32,128]{2,1,0:T(8,128)(2,1)} %shard_map.48), calls=%async_computation.1 | async-start | bytes 262144 | tf_op jit(solution)/shard_map/all_to_all | solution.py:306
  29.4 3.7 %shard_map.49.refs_0_ = bf16[704,768]{1,0:T(8,128)(2,1)} custom-call(bf16[512,768]{1,0:T(8,128)(2,1)} %refs_0_.3, bf16[512,768]{1,0:T(8,128)(2,1)} %refs_1_.3, bf16[512,768]{1,0:T(8,128)(2,1)} %refs_2_.4, bf16[704,768]{1,0:T(8,128)(2,1)} %shard_map.47.refs_3_), custom_call_target="tpu_custom_call", output_to_operand_aliasing={{}: (3, {})} | custom-call | flops 1073741824 | bytes 1310720 | tf_op jit(solution)/shard_map/pallas_call | solution.py:274
  33.1 0.9 %shard_map.50.o_ref = f32[16,32,128]{2,1,0:T(8,128)S(1)} custom-call(bf16[16,48,128]{2,1,0:T(8,128)(2,1)S(1)} %all-to-all-done.y_ref), custom_call_target="tpu_custom_call" | custom-call | tf_op jit(solution)/shard_map/pallas_call | solution.py:309
  34.0 0.0 copy-start
  34.0 0.0 copy-start.1
  34.0 2.8 %all-to-all-done.1.z_ref = bf16[16,32,128]{2,1,0:T(8,128)(2,1)S(1)} async-done(((bf16[16,32,128]{2,1,0:T(8,128)(2,1)}), bf16[16,32,128]{2,1,0:T(8,128)(2,1)S(1)}, u32[]{:S(2)}, u32[]{:S(2)}) %all-to-all-start.1) | async-done | bytes 131104 | tf_op jit(solution)/shard_map/all_to_all | solution.py:306
  36.7 0.6 %shard_map.51 = bf16[16,32,128]{2,1,0:T(8,128)(2,1)S(1)} custom-call(bf16[16,48,128]{2,1,0:T(8,128)(2,1)S(1)} %all-to-all-done.y_ref, bf16[16,32,128]{2,1,0:T(8,128)(2,1)S(1)} %all-to-all-done.1.z_ref, f32[16,32,128]{2,1,0:T(8,128)S(1)} %shard_map.50.o_ref), custom_call_target="tpu_custom_call" | custom-call | flops 10000000000 | bytes 1000000 | tf_op jit(solution)/shard_map/pallas_call | solution.py:311
  37.3 14.1 %all_to_all.15.refs_1_ = bf16[16,32,128]{2,1,0:T(8,128)(2,1)S(1)} all-to-all(bf16[16,32,128]{2,1,0:T(8,128)(2,1)S(1)} %shard_map.51), channel_id=1, replica_groups=mesh['row'=16,'col'=16] {'col'}, dimensions={0} | all-to-all | bytes 262144 | tf_op jit(solution)/shard_map/all_to_all | solution.py:316
  51.4 0.0 copy-done
  51.4 0.0 copy-done.1
  51.4 1.8 %shard_map.52 = bf16[512,768]{1,0:T(8,128)(2,1)} custom-call(bf16[704,768]{1,0:T(8,128)(2,1)S(1)} %copy-done, bf16[16,32,128]{2,1,0:T(8,128)(2,1)S(1)} %all_to_all.15.refs_1_, bf16[768,768]{1,0:T(8,128)(2,1)S(1)} %copy-done.1), custom_call_target="tpu_custom_call" | custom-call | tf_op jit(solution)/shard_map/pallas_call | solution.py:317
Async XLA Ops:
  2.8 17.6 %all-to-all-start = ((bf16[16,48,128]{2,1,0:T(8,128)(2,1)}), bf16[16,48,128]{2,1,0:T(8,128)(2,1)S(1)}, u32[]{:S(2)}, u32[]{:S(2)}) async-start(bf16[16,48,128]{2,1,0:T(8,128)(2,1)} %shard_map.46), calls=%async_computation | async-start | bytes 393216 | tf_op jit(solution)/shard_map/all_to_all | solution.py:295
  21.2 15.5 %all-to-all-start.1 = ((bf16[16,32,128]{2,1,0:T(8,128)(2,1)}), bf16[16,32,128]{2,1,0:T(8,128)(2,1)S(1)}, u32[]{:S(2)}, u32[]{:S(2)}) async-start(bf16[16,32,128]{2,1,0:T(8,128)(2,1)} %shard_map.48), calls=%async_computation.1 | async-start | bytes 262144 | tf_op jit(solution)/shard_map/all_to_all | solution.py:306
  34.0 17.4 %copy-start = (bf16[704,768]{1,0:T(8,128)(2,1)S(1)}, bf16[704,768]{1,0:T(8,128)(2,1)}, u32[]{:S(2)}) copy-start(bf16[704,768]{1,0:T(8,128)(2,1)} %shard_map.49.refs_0_) | copy-start | bytes 3244036
  34.0 17.4 %copy-start.1 = (bf16[768,768]{1,0:T(8,128)(2,1)S(1)}, bf16[768,768]{1,0:T(8,128)(2,1)}, u32[]{:S(2)}) copy-start(bf16[768,768]{1,0:T(8,128)(2,1)} %refs_2_.5) | copy-start | bytes 3538948

commit v4 on v3

--- a/solution.py
+++ b/solution.py
@@ -27,11 +27,28 @@
     return offset == head
 
 
+LOWER = (0, 3, 1, 2)
+UPPER = (3, 0, 2, 1)
+
+
 def slot_of(head, n_row, n_col):
     side = int(n_col**0.5)
+    low, high = LOWER[head // side], UPPER[head // side]
     upper = lax.div(lax.axis_index("row"), n_row // 2)
-    z = head // side
-    return (z + upper * (side - 1 - 2 * z)) * side + head % side
+    return (low + upper * (high - low)) * side + head % side
+
+
+def owner_groups(n_row, n_col):
+    side = int(n_col**0.5)
+    half = n_row // 2
+    groups = []
+    for low, high in zip(LOWER[:-1], UPPER[:-1]):
+        for y in range(side):
+            groups.append([r * n_col + (low if r < half else high) * side + y for r in range(n_row)])
+    for rows, z in ((range(half), LOWER[-1]), (range(half, n_row), UPPER[-1])):
+        for y in range(0, side, 2):
+            groups.append([r * n_col + z * side + y + i for i in range(2) for r in rows])
+    return groups
 
 
 def pack_kernel(period, n_row, q_hbm, k_hbm, v_hbm, x_ref, buf, sem):
@@ -234,15 +251,16 @@
         blocks.append(merge(out_a, lse_a, *remote[pair])[0])
     merged = jnp.concatenate(blocks, axis=1)
     keep = chosen_lanes(period, width)[None]
-    own = local[:rows, :].astype(F32).reshape(groups, period, width)
-    mixed = jnp.where(keep, merged[:, None, :], own).reshape(rows, width).astype(BF16)
     chunks = buf.shape[0]
-    wide = width // chunks
+    tall, wide = rows // chunks, groups // chunks
     copies = []
     for c in range(chunks):
-        part = pl.ds(c * wide, wide)
-        buf[c] = jnp.dot(mixed, w_ref[:, part], preferred_element_type=F32).astype(BF16)
-        copy = pltpu.make_async_copy(buf.at[c], out_hbm.at[:, part], out_sem.at[c])
+        part = slice(c * tall, c * tall + tall)
+        own = local[part, :].astype(F32).reshape(wide, period, width)
+        mixed = jnp.where(keep, merged[c * wide : c * wide + wide][:, None, :], own)
+        mixed = mixed.reshape(tall, width).astype(BF16)
+        buf[c] = jnp.dot(mixed, w_ref[...], preferred_element_type=F32).astype(BF16)
+        copy = pltpu.make_async_copy(buf.at[c], out_hbm.at[pl.ds(c * tall, tall)], out_sem.at[c])
         copy.start()
         copies.append(copy)
     for copy in copies:
@@ -298,11 +316,7 @@
     mine, first = lax.optimization_barrier((mine, first))
     top_own = call(middle_kernel, shape((n_row, 2 * n_col, 128), BF16))(mine)
     top_own, mine, first, *inputs = lax.optimization_barrier((top_own, mine, first, *inputs))
-    side = int(n_col**0.5)
-    owners = [
-        [r * n_col + (c if 2 * r < n_row else (side - 1 - c // side) * side + c % side) for r in range(n_row)]
-        for c in range(n_col)
-    ]
+    owners = owner_groups(n_row, n_col)
     top_all = lax.all_to_all(top_own, ("row", "col"), 0, 0, axis_index_groups=owners)
     second = local(early, HEADS // 2 - early, (*inputs, first), {3: 0})
     mine, second = lax.optimization_barrier((mine, second))
@@ -319,7 +333,7 @@
         shape((rows, width), BF16),
         in_specs=[whole] * 3,
         out_specs=anywhere,
-        scratch_shapes=[pltpu.VMEM((3, rows, width // 3), BF16), pltpu.SemaphoreType.DMA((3,))],
+        scratch_shapes=[pltpu.VMEM((4, rows // 4, width), BF16), pltpu.SemaphoreType.DMA((4,))],
     )(second, back, out_weight)
 
 

time: 53.5 us -> 52.6 us (0.983)
  blocking collectives: 14.1 us -> 13.2 us
    all_to_all x1, blocking collectives: 14.1 us -> 13.2 us  [shards(): back = lax.all_to_all(ret, 'col', 0, 0)]
  transfers between devices with their start and end apart: 2 -> 2, of which waited for: 2 -> 2; matrix products, arithmetic and copies ran while one was open for 0% -> 0% of each run, Pallas kernels for 19% -> 20%
where the time goes in v4:
time: 52.6 us; the launch traced here: 52.2 us
  starting transfers between devices  17.4 us (33%)
  Pallas kernels  16.1 us (31%)
  blocking collectives  13.2 us (25%)
  waiting for transfers between devices  5.43 us (10%)
    all_to_all x1, blocking collectives, shards(): back = lax.all_to_all(ret, 'col', 0, 0)  13.2 us
    pallas_call x2, Pallas kernels, local(): call(lambda *refs: local_kernel(start, *refs), shape((rows + 6 * groups,...  9.44 us
    all_to_all x1, starting transfers between devices, shards(): mine = lax.all_to_all(packed, 'col', 0, 0)  9.2 us
    all_to_all x1, starting transfers between devices, shards(): lax.all_to_all(top_own, ('row', 'col'), 0, 0, axis_index_groups=owners)  8.19 us
    pallas_call x1, Pallas kernels, shards(): call(lambda *refs: pack_kernel(n_col, n_row, *refs), shape((n_col, groups...  2.8 us
    all_to_all x1, waiting for transfers between devices, shards(): lax.all_to_all(top_own, ('row', 'col'), 0, 0, axis_index_groups=owners)  2.75 us
    all_to_all x1, waiting for transfers between devices, shards(): mine = lax.all_to_all(packed, 'col', 0, 0)  2.67 us
    pallas_call x1, Pallas kernels, shards(): call(lambda *refs: finish_kernel(n_col, n_row, *refs), shape((rows, width...  1.67 us
  transfers between devices with their start and end apart: 2, of which 2 were waited for; matrix products, arithmetic and copies ran while one was open for 0% of the time, Pallas kernels for 20%

profile of v4, /device:TPU:1, one launch (start us, length us, event | category | flops | bytes accessed | tf_op | source)
XLA Modules:
  0.0 52.2 jit_solution(5106818870485251857)
XLA Ops:
  0.0 2.8 %shard_map.46 = bf16[16,48,128]{2,1,0:T(8,128)(2,1)} custom-call(bf16[512,768]{1,0:T(8,128)(2,1)} %refs_0_.3, bf16[512,768]{1,0:T(8,128)(2,1)} %refs_1_.3, bf16[512,768]{1,0:T(8,128)(2,1)} %refs_2_.4), custom_call_target="tpu_custom_call" | custom-call | tf_op jit(solution)/shard_map/pallas_call | solution.py:283
  2.8 9.2 %all-to-all-start = ((bf16[16,48,128]{2,1,0:T(8,128)(2,1)}), bf16[16,48,128]{2,1,0:T(8,128)(2,1)S(1)}, u32[]{:S(2)}, u32[]{:S(2)}) async-start(bf16[16,48,128]{2,1,0:T(8,128)(2,1)} %shard_map.46), calls=%async_computation | async-start | bytes 393216 | tf_op jit(solution)/shard_map/all_to_all | solution.py:313
  12.0 5.7 %shard_map.47.refs_3_ = bf16[704,768]{1,0:T(8,128)(2,1)} custom-call(bf16[512,768]{1,0:T(8,128)(2,1)} %refs_0_.3, bf16[512,768]{1,0:T(8,128)(2,1)} %refs_1_.3, bf16[512,768]{1,0:T(8,128)(2,1)} %refs_2_.4), custom_call_target="tpu_custom_call" | custom-call | flops 2147483648 | bytes 2621440 | tf_op jit(solution)/shard_map/pallas_call | solution.py:292
  17.8 2.7 %all-to-all-done.y_ref = bf16[16,48,128]{2,1,0:T(8,128)(2,1)S(1)} async-done(((bf16[16,48,128]{2,1,0:T(8,128)(2,1)}), bf16[16,48,128]{2,1,0:T(8,128)(2,1)S(1)}, u32[]{:S(2)}, u32[]{:S(2)}) %all-to-all-start) | async-done | bytes 196640 | tf_op jit(solution)/shard_map/all_to_all | solution.py:313
  20.4 0.8 %shard_map.48 = bf16[16,32,128]{2,1,0:T(8,128)(2,1)} custom-call(bf16[16,48,128]{2,1,0:T(8,128)(2,1)S(1)} %all-to-all-done.y_ref), custom_call_target="tpu_custom_call" | custom-call | tf_op jit(solution)/shard_map/pallas_call | solution.py:317
  21.2 8.2 %all-to-all-start.1 = ((bf16[16,32,128]{2,1,0:T(8,128)(2,1)}), bf16[16,32,128]{2,1,0:T(8,128)(2,1)S(1)}, u32[]{:S(2)}, u32[]{:S(2)}) async-start(bf16[16,32,128]{2,1,0:T(8,128)(2,1)} %shard_map.48), calls=%async_computation.1 | async-start | bytes 262144 | tf_op jit(solution)/shard_map/all_to_all | solution.py:320
  29.4 3.7 %shard_map.49.refs_0_ = bf16[704,768]{1,0:T(8,128)(2,1)} custom-call(bf16[512,768]{1,0:T(8,128)(2,1)} %refs_0_.3, bf16[512,768]{1,0:T(8,128)(2,1)} %refs_1_.3, bf16[512,768]{1,0:T(8,128)(2,1)} %refs_2_.4, bf16[704,768]{1,0:T(8,128)(2,1)} %shard_map.47.refs_3_), custom_call_target="tpu_custom_call", output_to_operand_aliasing={{}: (3, {})} | custom-call | flops 1073741824 | bytes 1310720 | tf_op jit(solution)/shard_map/pallas_call | solution.py:292
  33.1 0.9 %shard_map.50.o_ref = f32[16,32,128]{2,1,0:T(8,128)S(1)} custom-call(bf16[16,48,128]{2,1,0:T(8,128)(2,1)S(1)} %all-to-all-done.y_ref), custom_call_target="tpu_custom_call" | custom-call | tf_op jit(solution)/shard_map/pallas_call | solution.py:323
  34.0 0.0 copy-start
  34.0 0.0 copy-start.1
  34.0 2.8 %all-to-all-done.1.z_ref = bf16[16,32,128]{2,1,0:T(8,128)(2,1)S(1)} async-done(((bf16[16,32,128]{2,1,0:T(8,128)(2,1)}), bf16[16,32,128]{2,1,0:T(8,128)(2,1)S(1)}, u32[]{:S(2)}, u32[]{:S(2)}) %all-to-all-start.1) | async-done | bytes 131104 | tf_op jit(solution)/shard_map/all_to_all | solution.py:320
  36.7 0.6 %shard_map.51 = bf16[16,32,128]{2,1,0:T(8,128)(2,1)S(1)} custom-call(bf16[16,48,128]{2,1,0:T(8,128)(2,1)S(1)} %all-to-all-done.y_ref, bf16[16,32,128]{2,1,0:T(8,128)(2,1)S(1)} %all-to-all-done.1.z_ref, f32[16,32,128]{2,1,0:T(8,128)S(1)} %shard_map.50.o_ref), custom_call_target="tpu_custom_call" | custom-call | flops 10000000000 | bytes 1000000 | tf_op jit(solution)/shard_map/pallas_call | solution.py:325
  37.3 13.2 %all_to_all.15.refs_1_ = bf16[16,32,128]{2,1,0:T(8,128)(2,1)S(1)} all-to-all(bf16[16,32,128]{2,1,0:T(8,128)(2,1)S(1)} %shard_map.51), channel_id=1, replica_groups=mesh['row'=16,'col'=16] {'col'}, dimensions={0} | all-to-all | bytes 262144 | tf_op jit(solution)/shard_map/all_to_all | solution.py:330
  50.5 0.0 copy-done
  50.5 0.0 copy-done.1
  50.5 1.7 %shard_map.52 = bf16[512,768]{1,0:T(8,128)(2,1)} custom-call(bf16[704,768]{1,0:T(8,128)(2,1)S(1)} %copy-done, bf16[16,32,128]{2,1,0:T(8,128)(2,1)S(1)} %all_to_all.15.refs_1_, bf16[768,768]{1,0:T(8,128)(2,1)S(1)} %copy-done.1), custom_call_target="tpu_custom_call" | custom-call | tf_op jit(solution)/shard_map/pallas_call | solution.py:331
Async XLA Ops:
  2.8 17.6 %all-to-all-start = ((bf16[16,48,128]{2,1,0:T(8,128)(2,1)}), bf16[16,48,128]{2,1,0:T(8,128)(2,1)S(1)}, u32[]{:S(2)}, u32[]{:S(2)}) async-start(bf16[16,48,128]{2,1,0:T(8,128)(2,1)} %shard_map.46), calls=%async_computation | async-start | bytes 393216 | tf_op jit(solution)/shard_map/all_to_all | solution.py:313
  21.2 15.5 %all-to-all-start.1 = ((bf16[16,32,128]{2,1,0:T(8,128)(2,1)}), bf16[16,32,128]{2,1,0:T(8,128)(2,1)S(1)}, u32[]{:S(2)}, u32[]{:S(2)}) async-start(bf16[16,32,128]{2,1,0:T(8,128)(2,1)} %shard_map.48), calls=%async_computation.1 | async-start | bytes 262144 | tf_op jit(solution)/shard_map/all_to_all | solution.py:320
  34.0 16.6 %copy-start = (bf16[704,768]{1,0:T(8,128)(2,1)S(1)}, bf16[704,768]{1,0:T(8,128)(2,1)}, u32[]{:S(2)}) copy-start(bf16[704,768]{1,0:T(8,128)(2,1)} %shard_map.49.refs_0_) | copy-start | bytes 3244036
  34.0 16.6 %copy-start.1 = (bf16[768,768]{1,0:T(8,128)(2,1)S(1)}, bf16[768,768]{1,0:T(8,128)(2,1)}, u32[]{:S(2)}) copy-start(bf16[768,768]{1,0:T(8,128)(2,1)} %refs_2_.5) | copy-start | bytes 3538948

commit v5 on v4

--- a/solution.py
+++ b/solution.py
@@ -31,9 +31,17 @@
 UPPER = (3, 0, 2, 1)
 
 
+ORDER = (1, 0, 2, 3)
+
+
+def col_order(n_col):
+    side = int(n_col**0.5)
+    return [[z * side + y for z in ORDER for y in range(side)]]
+
+
 def slot_of(head, n_row, n_col):
     side = int(n_col**0.5)
-    low, high = LOWER[head // side], UPPER[head // side]
+    low, high = ORDER.index(LOWER[head // side]), ORDER.index(UPPER[head // side])
     upper = lax.div(lax.axis_index("row"), n_row // 2)
     return (low + upper * (high - low)) * side + head % side
 
@@ -51,7 +59,7 @@
     return groups
 
 
-def pack_kernel(period, n_row, q_hbm, k_hbm, v_hbm, x_ref, buf, sem):
+def pack_kernel(period, n_row, q_hbm, k_hbm, v_hbm, x_hbm, buf, sem, x_ref, out_sem):
     rows, width = q_hbm.shape
     copies = [
         pltpu.make_async_copy(hbm, buf.at[i], sem.at[i])
@@ -60,6 +68,13 @@
     for copy in copies:
         copy.start()
     groups = rows // period
+    ends = (pl.ds(0, groups), pl.ds(groups, groups // 2))
+    sends = [
+        pltpu.make_async_copy(x_ref.at[:, part], x_hbm.at[:, part], out_sem.at[i])
+        for i, part in enumerate(ends)
+    ]
+    for rest in range(HEADS, x_ref.shape[0]):
+        x_ref[slot_of(rest, n_row, period)] = jnp.zeros(x_ref.shape[1:], BF16)
     keep = chosen_lanes(period, width).astype(BF16)
     member = (
         lax.broadcasted_iota(jnp.int32, (groups, rows), 1) // period
@@ -82,13 +97,15 @@
         qb, kb = q[:, lanes], k[:, lanes]
         x_ref[even, :groups] = jnp.where(low, qb, swap(kb)).astype(BF16)
         x_ref[odd, :groups] = jnp.where(low, swap(qb), kb).astype(BF16)
+    sends[0].start()
     v = pick(2)
     for lanes, even, odd in pairs:
         top, bottom = v[: groups // 2, lanes], v[groups // 2 :, lanes]
         x_ref[even, groups:] = jnp.where(low_half, top, swap(bottom)).astype(BF16)
         x_ref[odd, groups:] = jnp.where(low_half, swap(top), bottom).astype(BF16)
-    for rest in range(HEADS, x_ref.shape[0]):
-        x_ref[slot_of(rest, n_row, period)] = jnp.zeros(x_ref.shape[1:], BF16)
+    sends[1].start()
+    for send in sends:
+        send.wait()
 
 
 def middle_kernel(y_ref, z_ref):
@@ -285,7 +302,13 @@
         shape((n_col, groups * 3 // 2, 128), BF16),
         mib=56,
         in_specs=[distant] * 3,
-        scratch_shapes=[pltpu.VMEM((3, rows, width), BF16), pltpu.SemaphoreType.DMA((3,))],
+        out_specs=anywhere,
+        scratch_shapes=[
+            pltpu.VMEM((3, rows, width), BF16),
+            pltpu.SemaphoreType.DMA((3,)),
+            pltpu.VMEM((n_col, groups * 3 // 2, 128), BF16),
+            pltpu.SemaphoreType.DMA((2,)),
+        ],
     )(queries, keys, values)
     def local(start, count, inputs, aliases):
         pairs = rows * rows * 2 * count
@@ -310,7 +333,7 @@
 
     inputs = (queries, keys, values)
     packed, *inputs = lax.optimization_barrier((packed, *inputs))
-    mine = lax.all_to_all(packed, "col", 0, 0)
+    mine = lax.all_to_all(packed, "col", 0, 0, axis_index_groups=col_order(n_col))
     early = HEADS // 3
     first = local(0, early, inputs, {})
     mine, first = lax.optimization_barrier((mine, first))
@@ -327,7 +350,7 @@
         shape((n_col, groups, 128), BF16),
         cost_estimate=pl.CostEstimate(flops=10**10, bytes_accessed=10**6, transcendentals=0),
     )(mine, top_all, segment)
-    back = lax.all_to_all(ret, "col", 0, 0)
+    back = lax.all_to_all(ret, "col", 0, 0, axis_index_groups=col_order(n_col))
     return call(
         lambda *refs: finish_kernel(n_col, n_row, *refs),
         shape((rows, width), BF16),

time: 52.6 us -> 50.4 us (0.958)
  waiting for transfers between devices: 5.43 us -> 3.47 us
  blocking collectives: 13.2 us -> 11.8 us
  starting transfers between devices: 17.4 us -> 18.6 us
    all_to_all x1, waiting for transfers between devices: 2.67 us -> 0.71 us  [shards(): lax.all_to_all(packed, 'col', 0, 0, axis_index_groups=col_order(n_col))]
    all_to_all x1, blocking collectives: 13.2 us -> 11.8 us  [shards(): back = lax.all_to_all(ret, 'col', 0, 0, axis_index_groups=col_order(n_col))]
    all_to_all x1, starting transfers between devices: 8.19 us -> 9.2 us  [shards(): lax.all_to_all(top_own, ('row', 'col'), 0, 0, axis_index_groups=owners)]
  transfers between devices with their start and end apart: 2 -> 2, of which waited for: 2 -> 2; matrix products, arithmetic and copies ran while one was open for 0% -> 0% of each run, Pallas kernels for 20% -> 21%
where the time goes in v5:
time: 50.4 us; the launch traced here: 50 us
  starting transfers between devices  18.6 us (37%)
  Pallas kernels  16 us (32%)
  blocking collectives  11.8 us (23%)
  waiting for transfers between devices  3.47 us (7%)
    all_to_all x1, blocking collectives, shards(): back = lax.all_to_all(ret, 'col', 0, 0, axis_index_groups=col_order(n_col))  11.8 us
    pallas_call x2, Pallas kernels, local(): call(lambda *refs: local_kernel(start, *refs), shape((rows + 6 * groups,...  9.44 us
    all_to_all x1, starting transfers between devices, shards(): lax.all_to_all(packed, 'col', 0, 0, axis_index_groups=col_order(n_col))  9.39 us
    all_to_all x1, starting transfers between devices, shards(): lax.all_to_all(top_own, ('row', 'col'), 0, 0, axis_index_groups=owners)  9.2 us
    pallas_call x1, Pallas kernels, shards(): call(lambda *refs: pack_kernel(n_col, n_row, *refs), shape((n_col, groups...  2.76 us
    all_to_all x1, waiting for transfers between devices, shards(): lax.all_to_all(top_own, ('row', 'col'), 0, 0, axis_index_groups=owners)  2.75 us
    pallas_call x1, Pallas kernels, shards(): call(lambda *refs: finish_kernel(n_col, n_row, *refs), shape((rows, width...  1.67 us
  transfers between devices with their start and end apart: 2, of which 2 were waited for; matrix products, arithmetic and copies ran while one was open for 0% of the time, Pallas kernels for 21%

profile of v5, /device:TPU:1, one launch (start us, length us, event | category | flops | bytes accessed | tf_op | source)
XLA Modules:
  0.0 50.0 jit_solution(9179301826218423477)
XLA Ops:
  0.0 2.8 %shard_map.46 = bf16[16,48,128]{2,1,0:T(8,128)(2,1)} custom-call(bf16[512,768]{1,0:T(8,128)(2,1)} %refs_0_.3, bf16[512,768]{1,0:T(8,128)(2,1)} %refs_1_.3, bf16[512,768]{1,0:T(8,128)(2,1)} %refs_2_.4), custom_call_target="tpu_custom_call" | custom-call | tf_op jit(solution)/shard_map/pallas_call | solution.py:300
  2.8 9.4 %all-to-all-start = ((bf16[16,48,128]{2,1,0:T(8,128)(2,1)}), bf16[16,48,128]{2,1,0:T(8,128)(2,1)S(1)}, u32[]{:S(2)}, u32[]{:S(2)}) async-start(bf16[16,48,128]{2,1,0:T(8,128)(2,1)} %shard_map.46), calls=%async_computation | async-start | bytes 393216 | tf_op jit(solution)/shard_map/all_to_all | solution.py:336
  12.2 5.7 %shard_map.47.refs_3_ = bf16[704,768]{1,0:T(8,128)(2,1)} custom-call(bf16[512,768]{1,0:T(8,128)(2,1)} %refs_0_.3, bf16[512,768]{1,0:T(8,128)(2,1)} %refs_1_.3, bf16[512,768]{1,0:T(8,128)(2,1)} %refs_2_.4), custom_call_target="tpu_custom_call" | custom-call | flops 2147483648 | bytes 2621440 | tf_op jit(solution)/shard_map/pallas_call | solution.py:315
  17.9 0.7 %all-to-all-done.y_ref = bf16[16,48,128]{2,1,0:T(8,128)(2,1)S(1)} async-done(((bf16[16,48,128]{2,1,0:T(8,128)(2,1)}), bf16[16,48,128]{2,1,0:T(8,128)(2,1)S(1)}, u32[]{:S(2)}, u32[]{:S(2)}) %all-to-all-start) | async-done | bytes 196640 | tf_op jit(solution)/shard_map/all_to_all | solution.py:336
  18.6 0.8 %shard_map.48 = bf16[16,32,128]{2,1,0:T(8,128)(2,1)} custom-call(bf16[16,48,128]{2,1,0:T(8,128)(2,1)S(1)} %all-to-all-done.y_ref), custom_call_target="tpu_custom_call" | custom-call | tf_op jit(solution)/shard_map/pallas_call | solution.py:340
  19.4 9.2 %all-to-all-start.1 = ((bf16[16,32,128]{2,1,0:T(8,128)(2,1)}), bf16[16,32,128]{2,1,0:T(8,128)(2,1)S(1)}, u32[]{:S(2)}, u32[]{:S(2)}) async-start(bf16[16,32,128]{2,1,0:T(8,128)(2,1)} %shard_map.48), calls=%async_computation.1 | async-start | bytes 262144 | tf_op jit(solution)/shard_map/all_to_all | solution.py:343
  28.6 3.7 %shard_map.49.refs_0_ = bf16[704,768]{1,0:T(8,128)(2,1)} custom-call(bf16[512,768]{1,0:T(8,128)(2,1)} %refs_0_.3, bf16[512,768]{1,0:T(8,128)(2,1)} %refs_1_.3, bf16[512,768]{1,0:T(8,128)(2,1)} %refs_2_.4, bf16[704,768]{1,0:T(8,128)(2,1)} %shard_map.47.refs_3_), custom_call_target="tpu_custom_call", output_to_operand_aliasing={{}: (3, {})} | custom-call | flops 1073741824 | bytes 1310720 | tf_op jit(solution)/shard_map/pallas_call | solution.py:315
  32.3 0.9 %shard_map.50.o_ref = f32[16,32,128]{2,1,0:T(8,128)S(1)} custom-call(bf16[16,48,128]{2,1,0:T(8,128)(2,1)S(1)} %all-to-all-done.y_ref), custom_call_target="tpu_custom_call" | custom-call | tf_op jit(solution)/shard_map/pallas_call | solution.py:346
  33.1 0.0 copy-start
  33.2 0.0 copy-start.1
  33.2 2.8 %all-to-all-done.1.z_ref = bf16[16,32,128]{2,1,0:T(8,128)(2,1)S(1)} async-done(((bf16[16,32,128]{2,1,0:T(8,128)(2,1)}), bf16[16,32,128]{2,1,0:T(8,128)(2,1)S(1)}, u32[]{:S(2)}, u32[]{:S(2)}) %all-to-all-start.1) | async-done | bytes 131104 | tf_op jit(solution)/shard_map/all_to_all | solution.py:343
  35.9 0.6 %shard_map.51 = bf16[16,32,128]{2,1,0:T(8,128)(2,1)S(1)} custom-call(bf16[16,48,128]{2,1,0:T(8,128)(2,1)S(1)} %all-to-all-done.y_ref, bf16[16,32,128]{2,1,0:T(8,128)(2,1)S(1)} %all-to-all-done.1.z_ref, f32[16,32,128]{2,1,0:T(8,128)S(1)} %shard_map.50.o_ref), custom_call_target="tpu_custom_call" | custom-call | flops 10000000000 | bytes 1000000 | tf_op jit(solution)/shard_map/pallas_call | solution.py:348
  36.5 11.8 %all_to_all.15.refs_1_ = bf16[16,32,128]{2,1,0:T(8,128)(2,1)S(1)} all-to-all(bf16[16,32,128]{2,1,0:T(8,128)(2,1)S(1)} %shard_map.51), channel_id=1, replica_groups={{4,5,6,7,0,1,2,3,8,9,10,11,12,13,14,15},{20,21,22,23,16,17,18,19,24,25,..., dimensions={0} | all-to-all | bytes 262144 | tf_op jit(solution)/shard_map/all_to_all | solution.py:353
  48.3 0.0 copy-done
  48.3 0.0 copy-done.1
  48.3 1.7 %shard_map.52 = bf16[512,768]{1,0:T(8,128)(2,1)} custom-call(bf16[704,768]{1,0:T(8,128)(2,1)S(1)} %copy-done, bf16[16,32,128]{2,1,0:T(8,128)(2,1)S(1)} %all_to_all.15.refs_1_, bf16[768,768]{1,0:T(8,128)(2,1)S(1)} %copy-done.1), custom_call_target="tpu_custom_call" | custom-call | tf_op jit(solution)/shard_map/pallas_call | solution.py:354
Async XLA Ops:
  2.8 15.8 %all-to-all-start = ((bf16[16,48,128]{2,1,0:T(8,128)(2,1)}), bf16[16,48,128]{2,1,0:T(8,128)(2,1)S(1)}, u32[]{:S(2)}, u32[]{:S(2)}) async-start(bf16[16,48,128]{2,1,0:T(8,128)(2,1)} %shard_map.46), calls=%async_computation | async-start | bytes 393216 | tf_op jit(solution)/shard_map/all_to_all | solution.py:336
  19.4 16.6 %all-to-all-start.1 = ((bf16[16,32,128]{2,1,0:T(8,128)(2,1)}), bf16[16,32,128]{2,1,0:T(8,128)(2,1)S(1)}, u32[]{:S(2)}, u32[]{:S(2)}) async-start(bf16[16,32,128]{2,1,0:T(8,128)(2,1)} %shard_map.48), calls=%async_computation.1 | async-start | bytes 262144 | tf_op jit(solution)/shard_map/all_to_all | solution.py:343
  33.1 15.2 %copy-start = (bf16[704,768]{1,0:T(8,128)(2,1)S(1)}, bf16[704,768]{1,0:T(8,128)(2,1)}, u32[]{:S(2)}) copy-start(bf16[704,768]{1,0:T(8,128)(2,1)} %shard_map.49.refs_0_) | copy-start | bytes 3244036
  33.2 15.2 %copy-start.1 = (bf16[768,768]{1,0:T(8,128)(2,1)S(1)}, bf16[768,768]{1,0:T(8,128)(2,1)}, u32[]{:S(2)}) copy-start(bf16[768,768]{1,0:T(8,128)(2,1)} %refs_2_.5) | copy-start | bytes 3538948

commit v6 on v5

--- a/solution.py
+++ b/solution.py
@@ -52,7 +52,8 @@
     groups = []
     for low, high in zip(LOWER[:-1], UPPER[:-1]):
         for y in range(side):
-            groups.append([r * n_col + (low if r < half else high) * side + y for r in range(n_row)])
+            rows = [r ^ 1 for r in range(n_row)]
+            groups.append([r * n_col + (low if r < half else high) * side + y for r in rows])
     for rows, z in ((range(half), LOWER[-1]), (range(half, n_row), UPPER[-1])):
         for y in range(0, side, 2):
             groups.append([r * n_col + z * side + y + i for i in range(2) for r in rows])

time: 50.4 us -> 50.1 us (level)
  no operation moved by 1% of the time
where the time goes in v6:
time: 50.1 us; the launch traced here: 49.7 us
  starting transfers between devices  18.3 us (37%)
  Pallas kernels  16.1 us (32%)
  blocking collectives  11.8 us (24%)
  waiting for transfers between devices  3.44 us (7%)
    all_to_all x1, blocking collectives, shards(): back = lax.all_to_all(ret, 'col', 0, 0, axis_index_groups=col_order(n_col))  11.8 us
    pallas_call x2, Pallas kernels, local(): call(lambda *refs: local_kernel(start, *refs), shape((rows + 6 * groups,...  9.44 us
    all_to_all x1, starting transfers between devices, shards(): lax.all_to_all(packed, 'col', 0, 0, axis_index_groups=col_order(n_col))  9.39 us
    all_to_all x1, starting transfers between devices, shards(): lax.all_to_all(top_own, ('row', 'col'), 0, 0, axis_index_groups=owners)  8.9 us
    pallas_call x1, Pallas kernels, shards(): call(lambda *refs: pack_kernel(n_col, n_row, *refs), shape((n_col, groups...  2.76 us
    all_to_all x1, waiting for transfers between devices, shards(): lax.all_to_all(top_own, ('row', 'col'), 0, 0, axis_index_groups=owners)  2.73 us
    pallas_call x1, Pallas kernels, shards(): call(lambda *refs: finish_kernel(n_col, n_row, *refs), shape((rows, width...  1.67 us
  transfers between devices with their start and end apart: 2, of which 2 were waited for; matrix products, arithmetic and copies ran while one was open for 0% of the time, Pallas kernels for 21%

profile of v6, /device:TPU:1, one launch (start us, length us, event | category | flops | bytes accessed | tf_op | source)
XLA Modules:
  0.0 49.7 jit_solution(3500165330933024185)
XLA Ops:
  0.0 2.8 %shard_map.46 = bf16[16,48,128]{2,1,0:T(8,128)(2,1)} custom-call(bf16[512,768]{1,0:T(8,128)(2,1)} %refs_0_.3, bf16[512,768]{1,0:T(8,128)(2,1)} %refs_1_.3, bf16[512,768]{1,0:T(8,128)(2,1)} %refs_2_.4), custom_call_target="tpu_custom_call" | custom-call | tf_op jit(solution)/shard_map/pallas_call | solution.py:301
  2.8 9.4 %all-to-all-start = ((bf16[16,48,128]{2,1,0:T(8,128)(2,1)}), bf16[16,48,128]{2,1,0:T(8,128)(2,1)S(1)}, u32[]{:S(2)}, u32[]{:S(2)}) async-start(bf16[16,48,128]{2,1,0:T(8,128)(2,1)} %shard_map.46), calls=%async_computation | async-start | bytes 393216 | tf_op jit(solution)/shard_map/all_to_all | solution.py:337
  12.2 5.7 %shard_map.47.refs_3_ = bf16[704,768]{1,0:T(8,128)(2,1)} custom-call(bf16[512,768]{1,0:T(8,128)(2,1)} %refs_0_.3, bf16[512,768]{1,0:T(8,128)(2,1)} %refs_1_.3, bf16[512,768]{1,0:T(8,128)(2,1)} %refs_2_.4), custom_call_target="tpu_custom_call" | custom-call | flops 2147483648 | bytes 2621440 | tf_op jit(solution)/shard_map/pallas_call | solution.py:316
  17.9 0.7 %all-to-all-done.y_ref = bf16[16,48,128]{2,1,0:T(8,128)(2,1)S(1)} async-done(((bf16[16,48,128]{2,1,0:T(8,128)(2,1)}), bf16[16,48,128]{2,1,0:T(8,128)(2,1)S(1)}, u32[]{:S(2)}, u32[]{:S(2)}) %all-to-all-start) | async-done | bytes 196640 | tf_op jit(solution)/shard_map/all_to_all | solution.py:337
  18.6 0.8 %shard_map.48 = bf16[16,32,128]{2,1,0:T(8,128)(2,1)} custom-call(bf16[16,48,128]{2,1,0:T(8,128)(2,1)S(1)} %all-to-all-done.y_ref), custom_call_target="tpu_custom_call" | custom-call | tf_op jit(solution)/shard_map/pallas_call | solution.py:341
  19.4 8.9 %all-to-all-start.1 = ((bf16[16,32,128]{2,1,0:T(8,128)(2,1)}), bf16[16,32,128]{2,1,0:T(8,128)(2,1)S(1)}, u32[]{:S(2)}, u32[]{:S(2)}) async-start(bf16[16,32,128]{2,1,0:T(8,128)(2,1)} %shard_map.48), calls=%async_computation.1 | async-start | bytes 262144 | tf_op jit(solution)/shard_map/all_to_all | solution.py:344
  28.3 3.7 %shard_map.49.refs_0_ = bf16[704,768]{1,0:T(8,128)(2,1)} custom-call(bf16[512,768]{1,0:T(8,128)(2,1)} %refs_0_.3, bf16[512,768]{1,0:T(8,128)(2,1)} %refs_1_.3, bf16[512,768]{1,0:T(8,128)(2,1)} %refs_2_.4, bf16[704,768]{1,0:T(8,128)(2,1)} %shard_map.47.refs_3_), custom_call_target="tpu_custom_call", output_to_operand_aliasing={{}: (3, {})} | custom-call | flops 1073741824 | bytes 1310720 | tf_op jit(solution)/shard_map/pallas_call | solution.py:316
  32.0 0.9 %shard_map.50.o_ref = f32[16,32,128]{2,1,0:T(8,128)S(1)} custom-call(bf16[16,48,128]{2,1,0:T(8,128)(2,1)S(1)} %all-to-all-done.y_ref), custom_call_target="tpu_custom_call" | custom-call | tf_op jit(solution)/shard_map/pallas_call | solution.py:347
  32.9 0.0 copy-start
  32.9 0.0 copy-start.1
  32.9 2.7 %all-to-all-done.1.z_ref = bf16[16,32,128]{2,1,0:T(8,128)(2,1)S(1)} async-done(((bf16[16,32,128]{2,1,0:T(8,128)(2,1)}), bf16[16,32,128]{2,1,0:T(8,128)(2,1)S(1)}, u32[]{:S(2)}, u32[]{:S(2)}) %all-to-all-start.1) | async-done | bytes 131104 | tf_op jit(solution)/shard_map/all_to_all | solution.py:344
  35.6 0.6 %shard_map.51 = bf16[16,32,128]{2,1,0:T(8,128)(2,1)S(1)} custom-call(bf16[16,48,128]{2,1,0:T(8,128)(2,1)S(1)} %all-to-all-done.y_ref, bf16[16,32,128]{2,1,0:T(8,128)(2,1)S(1)} %all-to-all-done.1.z_ref, f32[16,32,128]{2,1,0:T(8,128)S(1)} %shard_map.50.o_ref), custom_call_target="tpu_custom_call" | custom-call | flops 10000000000 | bytes 1000000 | tf_op jit(solution)/shard_map/pallas_call | solution.py:349
  36.2 11.8 %all_to_all.15.refs_1_ = bf16[16,32,128]{2,1,0:T(8,128)(2,1)S(1)} all-to-all(bf16[16,32,128]{2,1,0:T(8,128)(2,1)S(1)} %shard_map.51), channel_id=1, replica_groups={{4,5,6,7,0,1,2,3,8,9,10,11,12,13,14,15},{20,21,22,23,16,17,18,19,24,25,..., dimensions={0} | all-to-all | bytes 262144 | tf_op jit(solution)/shard_map/all_to_all | solution.py:354
  48.0 0.0 copy-done
  48.0 0.0 copy-done.1
  48.0 1.7 %shard_map.52 = bf16[512,768]{1,0:T(8,128)(2,1)} custom-call(bf16[704,768]{1,0:T(8,128)(2,1)S(1)} %copy-done, bf16[16,32,128]{2,1,0:T(8,128)(2,1)S(1)} %all_to_all.15.refs_1_, bf16[768,768]{1,0:T(8,128)(2,1)S(1)} %copy-done.1), custom_call_target="tpu_custom_call" | custom-call | tf_op jit(solution)/shard_map/pallas_call | solution.py:355
Async XLA Ops:
  2.8 15.8 %all-to-all-start = ((bf16[16,48,128]{2,1,0:T(8,128)(2,1)}), bf16[16,48,128]{2,1,0:T(8,128)(2,1)S(1)}, u32[]{:S(2)}, u32[]{:S(2)}) async-start(bf16[16,48,128]{2,1,0:T(8,128)(2,1)} %shard_map.46), calls=%async_computation | async-start | bytes 393216 | tf_op jit(solution)/shard_map/all_to_all | solution.py:337
  19.4 16.2 %all-to-all-start.1 = ((bf16[16,32,128]{2,1,0:T(8,128)(2,1)}), bf16[16,32,128]{2,1,0:T(8,128)(2,1)S(1)}, u32[]{:S(2)}, u32[]{:S(2)}) async-start(bf16[16,32,128]{2,1,0:T(8,128)(2,1)} %shard_map.48), calls=%async_computation.1 | async-start | bytes 262144 | tf_op jit(solution)/shard_map/all_to_all | solution.py:344
  32.9 15.2 %copy-start = (bf16[704,768]{1,0:T(8,128)(2,1)S(1)}, bf16[704,768]{1,0:T(8,128)(2,1)}, u32[]{:S(2)}) copy-start(bf16[704,768]{1,0:T(8,128)(2,1)} %shard_map.49.refs_0_) | copy-start | bytes 3244036
  32.9 15.1 %copy-start.1 = (bf16[768,768]{1,0:T(8,128)(2,1)S(1)}, bf16[768,768]{1,0:T(8,128)(2,1)}, u32[]{:S(2)}) copy-start(bf16[768,768]{1,0:T(8,128)(2,1)} %refs_2_.5) | copy-start | bytes 3538948
